TPU v7x, 32 devices: a whole 2x2x4 slice. The times are simulated.
32 devices in a mesh: groups: 2 (over y), seq: 8 (over z, x), wt: 2 (over core).
Axes of the slice: x: 2, y: 2, z: 4, core: 2. Of those that a mesh axis runs over, the one named last changes fastest.
Arguments:
- query_input: bfloat16 [8192, 4096], P(('groups', 'seq'), 'wt'), parts along dimension 0, may hold values from -6 to 6
- key_input: bfloat16 [8192, 4096], P(('groups', 'seq'), 'wt'), parts along dimension 0, may hold values from -6 to 6
- value_input: bfloat16 [8192, 4096], P(('groups', 'seq'), 'wt'), parts along dimension 0, may hold values from -6 to 6
- gate_input: bfloat16 [8192, 4096], P(('groups', 'seq'), 'wt'), parts along dimension 0, may hold values from -6 to 6
- segment: int32 [8192], P(('groups', 'seq')), parts along dimension 0, may hold values from 0 to 7, never falling along the last dimension, each value on 1 to 1024 neighbouring positions
- decay_exponent: int32 [32], P('wt'), may hold values from 5 to 21
- retention: float32 [32, 8192], P('wt', ('groups', 'seq')), parts along dimension 1, may hold values from 0.5 to 1
- norm_gain: float32 [4096], P('wt'), may hold values from 0.5 to 1.5
Outputs:
- gated: bfloat16 [8192, 4096], P(('groups', 'seq'), 'wt'), parts along dimension 0
- snapshots: float32 [16, 32, 128, 128], P(('groups', 'seq'), 'wt'), parts along dimension 0
There are 2 independent parts, one for each index of `groups`. A program takes and returns all parts, laid end to end along the dimension named above; an argument that names none is the same for every part. Nothing has to cross between parts.
Inputs may be any that keep to these rules, and one draw needn't show every extreme that they name: `segment`: never falls along the slab and starts at 0.
All inputs are finite; a program needn't handle non-finite values.
Results may differ from a plain program's by a relative error of at most 0.0047.
Values sent between devices are 32-bit elements; how exact they have to be, the bound alone decides.
No kernel may reach another device: no remote copies, remote signals or barrier semaphores. Data moves between devices by JAX's collectives and lax.ppermute only.
A program may use at most 192 MiB of HBM per device.

v0:
```python
import functools

import jax
import jax.numpy as jnp
from jax import lax
from jax.experimental import pallas as pl
from jax.experimental.pallas import tpu as pltpu
from jax.sharding import PartitionSpec as P

F32 = jnp.float32
BF16 = jnp.bfloat16
NN = (((1,), (0,)), ((), ()))
NT = (((1,), (1,)), ((), ()))
MIB = 1 << 20
FIRST_LIMIT = 62 * MIB


def vmem_spec(shape, index_map):
    return pl.BlockSpec(shape, index_map)


def as_column(row, lanes):
    return jnp.broadcast_to(row, (lanes, row.shape[1])).T


def meta_rows(heads):
    return -(-(heads + 1) // 8) * 8


def put_message(msg_ref, first, heads, size, w_ref, finals, end, k_ref, v_ref):
    top = heads * size
    for j in range(heads):
        columns = slice(j * size, (j + 1) * size)
        weight = w_ref[first + j : first + j + 1, :]
        keyed = (k_ref[:, columns].astype(F32).T * weight).astype(BF16)
        msg_ref[columns, :] = lax.dot_general(
            keyed, v_ref[:, columns], NN, preferred_element_type=F32
        )
    msg_ref[top : top + heads, :] = jnp.broadcast_to(finals, (heads, size))
    below = meta_rows(heads) - heads
    msg_ref[top + heads :, :] = jnp.broadcast_to(end.astype(F32), (below, size))


def first_kernel(
    heads,
    chunk,
    seg_hbm,
    exponent_hbm,
    keep_hbm,
    k_hbm,
    v_hbm,
    msg_ref,
    a_ref,
    w_ref,
    seg_ref,
    exponent_ref,
    keep_ref,
    k_ref,
    v_ref,
    sems,
):
    tokens = seg_ref.shape[1]
    size = msg_ref.shape[1]
    wide = pl.ds(0, chunk * size)
    copies = [
        pltpu.make_async_copy(source, target, sems.at[i])
        for i, (source, target) in enumerate(
            [
                (keep_hbm, keep_ref),
                (exponent_hbm, exponent_ref),
                (seg_hbm, seg_ref),
                (k_hbm.at[:, wide], k_ref),
                (v_hbm.at[:, wide], v_ref),
            ]
        )
    ]
    for copy in copies:
        copy.start()
    earlier = lax.broadcasted_iota(jnp.int32, (tokens, tokens), 0)
    later = lax.broadcasted_iota(jnp.int32, (tokens, tokens), 1)
    upper = jnp.where(earlier <= later, 1.0, 0.0).astype(BF16)
    across = lax.broadcasted_iota(jnp.int32, (heads, heads), 1)
    down = lax.broadcasted_iota(jnp.int32, (heads, heads), 0)
    for copy in copies[:3]:
        copy.wait()
    spread = jnp.broadcast_to(exponent_ref[...], (heads, heads))
    exponent = jnp.sum(jnp.where(across == down, spread, 0).astype(F32), axis=1, keepdims=True)
    a = -jnp.exp2(-exponent) + jnp.log(keep_ref[...])
    high = a.astype(BF16)
    rest = a - high.astype(F32)
    middle = rest.astype(BF16)
    low = (rest - middle.astype(F32)).astype(BF16)
    parts = jnp.concatenate([high, middle, low], axis=0)
    sums = lax.dot_general(parts, upper, NN, preferred_element_type=F32)
    cumulative = sums[:heads] + (sums[heads : 2 * heads] + sums[2 * heads :])
    a_ref[...] = cumulative
    final = cumulative[:, tokens - 1 :]
    seg = seg_ref[...]
    last = seg[:, tokens - 1 :]
    w_ref[...] = jnp.where(seg == last, jnp.exp(final - cumulative), 0.0)
    for copy in copies[3:]:
        copy.wait()
    put_message(msg_ref, 0, chunk, size, w_ref, final[:chunk], last, k_ref, v_ref)


def first_message(seg, exponent, keep, k, v, heads, chunk):
    tokens, size = k.shape[0], k.shape[1] // heads
    rows = chunk * size + meta_rows(chunk)
    return pl.pallas_call(
        functools.partial(first_kernel, heads, chunk),
        in_specs=[pl.BlockSpec(memory_space=pltpu.HBM)] * 5,
        out_specs=[pl.BlockSpec(memory_space=pltpu.VMEM)] * 3,
        out_shape=[
            jax.ShapeDtypeStruct((rows, size), F32),
            jax.ShapeDtypeStruct((heads, tokens), F32),
            jax.ShapeDtypeStruct((heads, tokens), F32),
        ],
        scratch_shapes=[
            pltpu.VMEM((1, tokens), jnp.int32),
            pltpu.VMEM((1, heads), jnp.int32),
            pltpu.VMEM((heads, tokens), F32),
            pltpu.VMEM((tokens, chunk * size), BF16),
            pltpu.VMEM((tokens, chunk * size), BF16),
            pltpu.SemaphoreType.DMA((5,)),
        ],
        compiler_params=pltpu.CompilerParams(vmem_limit_bytes=FIRST_LIMIT),
        cost_estimate=pl.CostEstimate(
            flops=2 * tokens * chunk * size * size, bytes_accessed=2 * MIB, transcendentals=0
        ),
        name="first_message",
    )(seg, exponent, keep, k, v)


def next_kernel(
    first, heads, k_hbm, v_hbm, seg_ref, a_ref, w_ref, gate_ref, msg_ref, k_ref, v_ref, sems
):
    tokens = seg_ref.shape[1]
    size = msg_ref.shape[1]
    wide = pl.ds(first * size, heads * size)
    k_copy = pltpu.make_async_copy(k_hbm.at[:, wide], k_ref, sems.at[0])
    v_copy = pltpu.make_async_copy(v_hbm.at[:, wide], v_ref, sems.at[1])
    k_copy.start()
    v_copy.start()
    final = a_ref[first : first + heads, tokens - 1 :]
    last = seg_ref[:, tokens - 1 :]
    k_copy.wait()
    v_copy.wait()
    put_message(msg_ref, first, heads, size, w_ref, final, last, k_ref, v_ref)


def next_message(k, v, seg, a, w, gate, first, heads):
    tokens, size = k.shape[0], k.shape[1] // a.shape[0]
    rows = heads * size + meta_rows(heads)
    return pl.pallas_call(
        functools.partial(next_kernel, first, heads),
        in_specs=[pl.BlockSpec(memory_space=pltpu.HBM)] * 2
        + [pl.BlockSpec(memory_space=pltpu.VMEM)] * 3
        + [pl.BlockSpec(memory_space=pl.ANY)],
        out_specs=pl.BlockSpec(memory_space=pltpu.VMEM),
        out_shape=jax.ShapeDtypeStruct((rows, size), F32),
        scratch_shapes=[
            pltpu.VMEM((tokens, heads * size), BF16),
            pltpu.VMEM((tokens, heads * size), BF16),
            pltpu.SemaphoreType.DMA((2,)),
        ],
        compiler_params=pltpu.CompilerParams(vmem_limit_bytes=16 * MIB),
        cost_estimate=pl.CostEstimate(
            flops=2 * tokens * heads * size * size, bytes_accessed=2 * MIB, transcendentals=0
        ),
        name="next_message",
    )(k, v, seg, a, w, gate)


def join_kernel(heads, order_ref, mine_ref, other_ref, *rest):
    out_ref = rest[-1]
    size = mine_ref.shape[1]
    top = heads * size
    mine_later = order_ref[0] == 1
    final_mine, final_other = mine_ref[top : top + heads, :], other_ref[top : top + heads, :]
    end_mine, end_other = mine_ref[top + heads :, :], other_ref[top + heads :, :]
    same = jnp.where(end_mine[:1] == end_other[:1], 1.0, 0.0)
    scale_mine = jnp.where(mine_later, 1.0, jnp.exp(final_other) * same)
    scale_other = jnp.where(mine_later, jnp.exp(final_mine) * same, 1.0)
    for head in range(heads):
        rows = slice(head * size, (head + 1) * size)
        out_ref[rows, :] = (
            scale_mine[head : head + 1] * mine_ref[rows, :]
            + scale_other[head : head + 1] * other_ref[rows, :]
        )
    out_ref[top : top + heads, :] = final_mine + final_other
    out_ref[top + heads :, :] = jnp.where(mine_later, end_mine, end_other)


def joined(order, mine, other, heads, after=()):
    rows, size = mine.shape
    return pl.pallas_call(
        functools.partial(join_kernel, heads),
        in_specs=[pl.BlockSpec(memory_space=pltpu.SMEM)]
        + [pl.BlockSpec(memory_space=pltpu.VMEM)] * 2
        + [pl.BlockSpec(memory_space=pl.ANY)] * len(after),
        out_specs=pl.BlockSpec(memory_space=pltpu.VMEM),
        out_shape=jax.ShapeDtypeStruct((rows, size), F32),
        compiler_params=pltpu.CompilerParams(vmem_limit_bytes=16 * MIB),
        cost_estimate=pl.CostEstimate(
            flops=3 * rows * size, bytes_accessed=12 * rows * size, transcendentals=0
        ),
        name="join_windows",
    )(order, mine, other, *after)


def make_mask(seg_ref, mask_ref):
    tokens = seg_ref.shape[1]
    seg = seg_ref[...].astype(F32)
    column = as_column(seg, 128)
    for start in range(0, tokens, 128):
        across = lax.broadcasted_iota(jnp.int32, (tokens, 128), 1) + start
        down = lax.broadcasted_iota(jnp.int32, (tokens, 128), 0)
        seen = (column == seg[:, start : start + 128]) & (across <= down)
        mask_ref[:, start : start + 128] = jnp.where(seen, 0.0, -1e30)


def intra_kernel(
    first, heads, seg_ref, a_ref, q_hbm, k_hbm, v_hbm, o_ref, mask_ref, q_ref, k_ref, v_ref, sems
):
    tokens = seg_ref.shape[1]
    size = q_ref.shape[1] // heads
    block = min(tokens, 256)
    wide = pl.ds(first * size, heads * size)
    copies = [
        pltpu.make_async_copy(source.at[:, wide], target, sems.at[i])
        for i, (source, target) in enumerate([(q_hbm, q_ref), (k_hbm, k_ref), (v_hbm, v_ref)])
    ]
    for copy in copies:
        copy.start()
    make_mask(seg_ref, mask_ref)
    for copy in copies:
        copy.wait()
    for j in range(heads):
        columns = slice(j * size, (j + 1) * size)
        a_row = a_ref[first + j : first + j + 1, :] * 1.4426950408889634
        a_column = as_column(a_row, 128)
        for start in range(0, tokens, block):
            here, upto = slice(start, start + block), slice(0, start + block)
            scores = lax.dot_general(
                q_ref[here, columns], k_ref[upto, columns], NT, preferred_element_type=F32
            )
            spread = jnp.concatenate([a_column[here]] * ((start + block) // 128), axis=1)
            weight = jnp.exp2(spread - a_row[:, upto] + mask_ref[here, upto])
            probs = (scores * weight).astype(BF16)
            o_ref[here, columns] = lax.dot_general(
                probs, v_ref[upto, columns], NN, preferred_element_type=F32
            )


def intra(seg, a, q, k, v, first, heads):
    tokens, size = k.shape[0], k.shape[1] // a.shape[0]
    return pl.pallas_call(
        functools.partial(intra_kernel, first, heads),
        in_specs=[pl.BlockSpec(memory_space=pltpu.VMEM)] * 2
        + [pl.BlockSpec(memory_space=pltpu.HBM)] * 3,
        out_specs=pl.BlockSpec(memory_space=pltpu.VMEM),
        out_shape=jax.ShapeDtypeStruct((tokens, heads * size), F32),
        scratch_shapes=[pltpu.VMEM((tokens, tokens), F32)]
        + [pltpu.VMEM((tokens, heads * size), BF16)] * 3
        + [pltpu.SemaphoreType.DMA((3,))],
        compiler_params=pltpu.CompilerParams(vmem_limit_bytes=24 * MIB),
        cost_estimate=pl.CostEstimate(
            flops=3 * tokens * tokens * heads * size,
            bytes_accessed=3 * MIB,
            transcendentals=tokens * tokens * heads,
        ),
        name="intra_span",
    )(seg, a, q, k, v)


def final_kernel(
    first,
    heads,
    order_ref,
    seg_ref,
    a_ref,
    own_ref,
    pair_ref,
    before_ref,
    o_ref,
    gain_ref,
    q_ref,
    g_ref,
    *rest,
):
    gated_ref, snap_ref, token_ref = rest[-3:]
    token_ref[...] = jnp.zeros_like(token_ref)
    size = own_ref.shape[1]
    top = heads * size
    second = order_ref[0] == 1
    ends = slice(top + heads, top + heads + 1)
    finals = slice(top, top + heads)
    own_end, pair_end, before_end = own_ref[ends, :], pair_ref[ends, :], before_ref[ends, :]
    previous = jnp.where(second, pair_end, before_end)
    kept = jnp.where(own_end == previous, 1.0, 0.0)
    bridged = jnp.where(pair_end == before_end, 1.0, 0.0)
    own_decay = jnp.exp(own_ref[finals, :]) * kept
    from_before = jnp.where(second, jnp.exp(pair_ref[finals, :]) * bridged, 1.0)
    from_pair = jnp.where(second, 1.0, 0.0)
    valid = seg_ref[...].astype(F32) == previous[:, :1]
    for j in range(heads):
        rows = columns = slice(j * size, (j + 1) * size)
        state = from_before[j : j + 1] * before_ref[rows, :] + from_pair * pair_ref[rows, :]
        snap_ref[0, j] = own_decay[j : j + 1] * state + own_ref[rows, :]
        high = state.astype(BF16)
        low = (state - high.astype(F32)).astype(BF16)
        q = q_ref[:, columns]
        inter = lax.dot_general(
            jnp.concatenate([q, q], axis=1),
            jnp.concatenate([high, low], axis=0),
            NN,
            preferred_element_type=F32,
        )
        decay = jnp.where(valid, jnp.exp(a_ref[first + j : first + j + 1, :]), 0.0)
        mixed = o_ref[:, columns] + inter * as_column(decay, size)
        mean_square = jnp.mean(mixed * mixed, axis=1, keepdims=True)
        g = g_ref[:, columns].astype(F32)
        gain = gain_ref[:, columns]
        gated = mixed * lax.rsqrt(mean_square + 1e-06) * gain / (1.0 + jnp.exp(-g))
        gated_ref[:, columns] = gated.astype(BF16)


def finish(order, seg, a, own, pair, before, o, gain, q, g, so_far, first, heads):
    tokens, total = q.shape[0], a.shape[0]
    size = q.shape[1] // total
    place = first // heads
    wide = lambda rows: pl.BlockSpec((rows, heads * size), lambda i: (0, place))
    vmem = pl.BlockSpec(memory_space=pltpu.VMEM)
    return pl.pallas_call(
        functools.partial(final_kernel, first, heads),
        grid=(1,),
        in_specs=[pl.BlockSpec(memory_space=pltpu.SMEM)]
        + [vmem] * 6
        + [wide(1), wide(tokens), wide(tokens)]
        + [pl.BlockSpec(memory_space=pl.ANY)] * len(so_far),
        out_specs=[
            wide(tokens),
            pl.BlockSpec((1, heads, size, size), lambda i: (0, place, 0, 0)),
            vmem,
        ],
        out_shape=[
            jax.ShapeDtypeStruct((tokens, total * size), BF16),
            jax.ShapeDtypeStruct((1, total, size, size), F32),
            jax.ShapeDtypeStruct((8, 128), F32),
        ],
        input_output_aliases={10 + i: i for i in range(len(so_far))},
        compiler_params=pltpu.CompilerParams(vmem_limit_bytes=24 * MIB),
        cost_estimate=pl.CostEstimate(
            flops=4 * tokens * heads * size * size,
            bytes_accessed=4 * MIB,
            transcendentals=2 * tokens * heads * size,
        ),
        name="finish",
    )(order, seg, a, own, pair, before, o, gain, q, g, *so_far)


def shards(q, k, v, g, segment, decay_exponent, retention, norm_gain):
    heads = decay_exponent.shape[0]
    tokens = q.shape[0]
    count = lax.axis_size("seq")
    place = lax.axis_index("seq")
    reach = max(1, count // 4)
    chunk = 4
    firsts = list(range(0, heads, chunk))
    seg = segment.reshape(1, tokens)
    gain = norm_gain.reshape(1, -1)
    order = lax.rem(place, 2).astype(jnp.int32).reshape(1)
    swap = [(c, c ^ 1) for c in range(count)]

    own, pair, both, before, o = {}, {}, {}, {}, {}
    tokens_of, so_far = {}, ()
    own[0], a, w = first_message(seg, decay_exponent.reshape(1, heads), retention, k, v, heads, chunk)
    pair[0] = lax.ppermute(own[0], "seq", swap)
    own[1] = next_message(k, v, seg, a, w, w, firsts[1], chunk)
    pair[1] = lax.ppermute(own[1], "seq", swap)
    for i, first in enumerate(firsts):
        o[i] = intra(seg, a, q, k, v, first, chunk)
        after = (o[i],) + ((tokens_of[i - 2],) if i > 1 else ())
        both[i] = joined(order, own[i], pair[i], chunk, after)
        before[i] = lax.ppermute(both[i], "seq", [(c, c + 2) for c in range(count - 2)])
        window = 2
        while window < reach:
            far = lax.ppermute(before[i], "seq", [(c, c + window) for c in range(count - window)])
            before[i] = joined(jnp.ones((1,), jnp.int32), before[i], far, chunk)
            window *= 2
        if i + 2 < len(firsts):
            own[i + 2] = next_message(k, v, seg, a, w, both[i], firsts[i + 2], chunk)
            pair[i + 2] = lax.ppermute(own[i + 2], "seq", swap)
        *so_far, tokens_of[i] = finish(
            order, seg, a, own[i], pair[i], before[i], o[i], gain, q, g, so_far, first, chunk
        )
    return tuple(so_far)


def solution(mesh):
    placed = (
        P(("groups", "seq"), "wt"),
        P(("groups", "seq"), "wt"),
        P(("groups", "seq"), "wt"),
        P(("groups", "seq"), "wt"),
        P(("groups", "seq")),
        P("wt"),
        P("wt", ("groups", "seq")),
        P("wt"),
    )
    return jax.shard_map(
        shards,
        mesh=mesh,
        in_specs=placed,
        out_specs=(P(("groups", "seq"), "wt"), P(("groups", "seq"), "wt", None, None)),
        check_vma=False,
    )
```

profile of v0, /device:TPU:0, one launch (start us, length us, event | category | flops | bytes accessed | tf_op | source)
XLA Modules:
  0.0 50.4 jit_solution(4970702220129606608)
XLA Ops:
  0.6 2.4 %first_message.1 = (f32[520,128]{1,0:T(8,128)}, f32[16,512]{1,0:T(8,128)}, f32[16,512]{1,0:T(8,128)}) custom-call(s32[1,512]{1,0:T(1,128)} %bitcast.4, s32[1,16]{1,0:T(1,128)} %bitcast.20, f32[16,512]{1,0:T(8,128)} %keep_hbm.1, bf16[512,2048]{1,0:T(8,128)(2,1)} %k_hbm.15, bf16[512,2048]{1,0:T(8,128)(2,1)} %v_hbm.15), custom_call_target="tpu_custom_call" | custom-call | flops 67108864 | bytes 2097152 | tf_op jit(solution)/shard_map/first_message/pallas_call | solution.py:109
  3.0 3.0 %collective-permute-start.3 = (f32[520,128]{1,0:T(8,128)}, f32[520,128]{1,0:T(8,128)S(1)}, u32[]{:S(2)}, u32[]{:S(2)}) collective-permute-start(f32[520,128]{1,0:T(8,128)} %get-tuple-element.17.mine_ref.own_ref), channel_id=1, source_target_pairs={{0,2},{2,0},{4,6},{6,4},{8,10},{10,8},{12,14},{14,12},{1,3},{3,1},... | collective-permute-start | bytes 798728 | tf_op jit(solution)/shard_map/ppermute | solution.py:378
  6.0 1.6 %copy-done.1 = bf16[512,2048]{1,0:T(8,128)(2,1)S(1)} copy-done((bf16[512,2048]{1,0:T(8,128)(2,1)S(1)}, bf16[512,2048]{1,0:T(8,128)(2,1)}, u32[]{:S(2)}) %copy-start.1) | copy-done | bytes 2097176
  7.6 1.6 %copy-done.3 = bf16[512,2048]{1,0:T(8,128)(2,1)S(1)} copy-done((bf16[512,2048]{1,0:T(8,128)(2,1)S(1)}, bf16[512,2048]{1,0:T(8,128)(2,1)}, u32[]{:S(2)}) %copy-start.3) | copy-done | bytes 2097176
  9.2 0.8 %copy-done.6 = f32[16,512]{1,0:T(8,128)S(1)} copy-done((f32[16,512]{1,0:T(8,128)S(1)}, f32[16,512]{1,0:T(8,128)}, u32[]{:S(2)}) %copy-start.6) | copy-done | bytes 32792
  11.4 1.0 %copy-done = bf16[512,2048]{1,0:T(8,128)(2,1)S(1)} copy-done((bf16[512,2048]{1,0:T(8,128)(2,1)S(1)}, bf16[512,2048]{1,0:T(8,128)(2,1)}, u32[]{:S(2)}) %copy-start) | copy-done | bytes 2097176
  12.3 1.6 %copy-done.2 = bf16[512,2048]{1,0:T(8,128)(2,1)S(1)} copy-done((bf16[512,2048]{1,0:T(8,128)(2,1)S(1)}, bf16[512,2048]{1,0:T(8,128)(2,1)}, u32[]{:S(2)}) %copy-start.2) | copy-done | bytes 2097176
  13.9 1.6 %copy-done.4 = bf16[512,2048]{1,0:T(8,128)(2,1)S(1)} copy-done((bf16[512,2048]{1,0:T(8,128)(2,1)S(1)}, bf16[512,2048]{1,0:T(8,128)(2,1)}, u32[]{:S(2)}) %copy-start.4) | copy-done | bytes 2097176
  15.5 1.8 %intra_span.6.rest_0_.o_ref = f32[512,512]{1,0:T(8,128)S(1)} custom-call(s32[1,512]{1,0:T(1,128)S(1)} %bitcast.6, f32[16,512]{1,0:T(8,128)S(1)} %copy-done.7, bf16[512,2048]{1,0:T(8,128)(2,1)S(1)} %copy-done, bf16[512,2048]{1,0:T(8,128)(2,1)S(1)} %copy-done.2, bf16[512,2048]{1,0:T(8,128)(2,1)S(1)} %copy-done.4), custom_call_target="tpu_custom_call" | custom-call | flops 402653184 | bytes 3145728 | tf_op jit(solution)/shard_map/intra_span/pallas_call | solution.py:257
  17.4 3.5 %collective-permute-start.4 = (f32[520,128]{1,0:T(8,128)S(1)}, f32[520,128]{1,0:T(8,128)S(1)}, u32[]{:S(2)}, u32[]{:S(2)}) collective-permute-start(f32[520,128]{1,0:T(8,128)S(1)} %join_windows.5.gate_ref), channel_id=1, source_target_pairs={{0,4},{2,6},{4,8},{6,10},{8,12},{10,14},{1,5},{3,7},{5,9},{7,11},{... | collective-permute-start | bytes 798728 | tf_op jit(solution)/shard_map/ppermute | solution.py:385
  21.5 1.1 %collective-permute-start.6 = (f32[520,128]{1,0:T(8,128)S(1)}, f32[520,128]{1,0:T(8,128)S(1)}, u32[]{:S(2)}, u32[]{:S(2)}) collective-permute-start(f32[520,128]{1,0:T(8,128)S(1)} %next_message.5.mine_ref.own_ref), channel_id=1, source_target_pairs={{0,2},{2,0},{4,6},{6,4},{8,10},{10,8},{12,14},{14,12},{1,3},{3,1},... | collective-permute-start | bytes 798728 | tf_op jit(solution)/shard_map/ppermute | solution.py:393
  22.6 1.8 %intra_span.4.rest_0_.o_ref = f32[512,512]{1,0:T(8,128)S(1)} custom-call(s32[1,512]{1,0:T(1,128)S(1)} %bitcast.8, f32[16,512]{1,0:T(8,128)S(1)} %copy-done.7, bf16[512,2048]{1,0:T(8,128)(2,1)S(1)} %copy-done, bf16[512,2048]{1,0:T(8,128)(2,1)S(1)} %copy-done.2, bf16[512,2048]{1,0:T(8,128)(2,1)S(1)} %copy-done.4), custom_call_target="tpu_custom_call" | custom-call | flops 402653184 | bytes 3145728 | tf_op jit(solution)/shard_map/intra_span/pallas_call | solution.py:257
  24.5 3.5 %collective-permute-start.2 = (f32[520,128]{1,0:T(8,128)S(1)}, f32[520,128]{1,0:T(8,128)S(1)}, u32[]{:S(2)}, u32[]{:S(2)}) collective-permute-start(f32[520,128]{1,0:T(8,128)S(1)} %join_windows.4.gate_ref), channel_id=1, source_target_pairs={{0,4},{2,6},{4,8},{6,10},{8,12},{10,14},{1,5},{3,7},{5,9},{7,11},{... | collective-permute-start | bytes 798728 | tf_op jit(solution)/shard_map/ppermute | solution.py:385
  28.5 1.1 %collective-permute-start.1 = (f32[520,128]{1,0:T(8,128)S(1)}, f32[520,128]{1,0:T(8,128)S(1)}, u32[]{:S(2)}, u32[]{:S(2)}) collective-permute-start(f32[520,128]{1,0:T(8,128)S(1)} %next_message.4.mine_ref.own_ref), channel_id=1, source_target_pairs={{0,2},{2,0},{4,6},{6,4},{8,10},{10,8},{12,14},{14,12},{1,3},{3,1},... | collective-permute-start | bytes 798728 | tf_op jit(solution)/shard_map/ppermute | solution.py:393
  29.6 1.9 %intra_span.5.rest_0_.o_ref = f32[512,512]{1,0:T(8,128)S(1)} custom-call(s32[1,512]{1,0:T(1,128)S(1)} %bitcast.10, f32[16,512]{1,0:T(8,128)S(1)} %copy-done.7, bf16[512,2048]{1,0:T(8,128)(2,1)S(1)} %copy-done, bf16[512,2048]{1,0:T(8,128)(2,1)S(1)} %copy-done.2, bf16[512,2048]{1,0:T(8,128)(2,1)S(1)} %copy-done.4), custom_call_target="tpu_custom_call" | custom-call | flops 402653184 | bytes 3145728 | tf_op jit(solution)/shard_map/intra_span/pallas_call | solution.py:257
  31.5 1.9 %intra_span.7.rest_0_.o_ref = f32[512,512]{1,0:T(8,128)S(1)} custom-call(s32[1,512]{1,0:T(1,128)S(1)} %bitcast.11, f32[16,512]{1,0:T(8,128)S(1)} %copy-done.7, bf16[512,2048]{1,0:T(8,128)(2,1)S(1)} %copy-done, bf16[512,2048]{1,0:T(8,128)(2,1)S(1)} %copy-done.2, bf16[512,2048]{1,0:T(8,128)(2,1)S(1)} %copy-done.4), custom_call_target="tpu_custom_call" | custom-call | flops 402653184 | bytes 3145728 | tf_op jit(solution)/shard_map/intra_span/pallas_call | solution.py:257
  33.4 1.8 %finish.4 = (bf16[512,2048]{1,0:T(8,128)(2,1)}, f32[1,16,128,128]{3,2,1,0:T(8,128)}, f32[8,128]{1,0:T(8,128)S(1)}) custom-call(s32[1]{0:T(128)} %bitcast.order_ref, s32[1,512]{1,0:T(1,128)S(1)} %bitcast.12, f32[16,512]{1,0:T(8,128)S(1)} %copy-done.7, f32[520,128]{1,0:T(8,128)S(1)} %copy-done.8, f32[520,128]{1,0:T(8,128)S(1)} %collective-permute-done.3.other_ref.pair_ref, ...), custom_call_target="tpu_custom_call" | custom-call | flops 134217728 | bytes 4194304 | tf_op jit(solution)/shard_map/finish/pallas_call | solution.py:334
  35.3 3.5 %collective-permute-start.7 = (f32[520,128]{1,0:T(8,128)S(1)}, f32[520,128]{1,0:T(8,128)S(1)}, u32[]{:S(2)}, u32[]{:S(2)}) collective-permute-start(f32[520,128]{1,0:T(8,128)S(1)} %join_windows.7), channel_id=1, source_target_pairs={{0,4},{2,6},{4,8},{6,10},{8,12},{10,14},{1,5},{3,7},{5,9},{7,11},{... | collective-permute-start | bytes 798728 | tf_op jit(solution)/shard_map/ppermute | solution.py:385
  38.7 1.8 %finish.5 = (bf16[512,2048]{1,0:T(8,128)(2,1)}, f32[1,16,128,128]{3,2,1,0:T(8,128)}, f32[8,128]{1,0:T(8,128)S(1)}) custom-call(s32[1]{0:T(128)} %bitcast.order_ref, s32[1,512]{1,0:T(1,128)S(1)} %bitcast.13, f32[16,512]{1,0:T(8,128)S(1)} %copy-done.7, f32[520,128]{1,0:T(8,128)S(1)} %next_message.3.mine_ref.own_ref, ...), custom_call_target="tpu_custom_call", output_to_operand_aliasing={{0}: (10, {}), {1}: (11, {})} | custom-call | flops 134217728 | bytes 4194304 | tf_op jit(solution)/shard_map/finish/pallas_call | solution.py:334
  40.6 1.9 %collective-permute-start.5 = (f32[520,128]{1,0:T(8,128)S(1)}, f32[520,128]{1,0:T(8,128)S(1)}, u32[]{:S(2)}, u32[]{:S(2)}) collective-permute-start(f32[520,128]{1,0:T(8,128)S(1)} %join_windows.6), channel_id=1, source_target_pairs={{0,4},{2,6},{4,8},{6,10},{8,12},{10,14},{1,5},{3,7},{5,9},{7,11},{... | collective-permute-start | bytes 798728 | tf_op jit(solution)/shard_map/ppermute | solution.py:385
  42.5 2.3 %collective-permute-done.7.before_ref = f32[520,128]{1,0:T(8,128)S(1)} collective-permute-done((f32[520,128]{1,0:T(8,128)S(1)}, f32[520,128]{1,0:T(8,128)S(1)}, u32[]{:S(2)}, u32[]{:S(2)}) %collective-permute-start.7) | collective-permute-done | bytes 266272 | tf_op jit(solution)/shard_map/ppermute | solution.py:385
  44.8 1.8 %finish.6 = (bf16[512,2048]{1,0:T(8,128)(2,1)}, f32[1,16,128,128]{3,2,1,0:T(8,128)}, f32[8,128]{1,0:T(8,128)}) custom-call(s32[1]{0:T(128)} %bitcast.order_ref, s32[1,512]{1,0:T(1,128)S(1)} %bitcast.14, f32[16,512]{1,0:T(8,128)S(1)} %copy-done.7, f32[520,128]{1,0:T(8,128)S(1)} %next_message.5.mine_ref.own_ref, ...), custom_call_target="tpu_custom_call", output_to_operand_aliasing={{0}: (10, {}), {1}: (11, {})} | custom-call | flops 134217728 | bytes 4194304 | tf_op jit(solution)/shard_map/finish/pallas_call | solution.py:334
  46.6 2.1 %collective-permute-done.5.before_ref = f32[520,128]{1,0:T(8,128)S(1)} collective-permute-done((f32[520,128]{1,0:T(8,128)S(1)}, f32[520,128]{1,0:T(8,128)S(1)}, u32[]{:S(2)}, u32[]{:S(2)}) %collective-permute-start.5) | collective-permute-done | bytes 266272 | tf_op jit(solution)/shard_map/ppermute | solution.py:385
  48.6 1.8 %finish.7 = (bf16[512,2048]{1,0:T(8,128)(2,1)}, f32[1,16,128,128]{3,2,1,0:T(8,128)}, f32[8,128]{1,0:T(8,128)}) custom-call(s32[1]{0:T(128)} %bitcast.order_ref, s32[1,512]{1,0:T(1,128)S(1)} %bitcast.15, f32[16,512]{1,0:T(8,128)S(1)} %copy-done.7, f32[520,128]{1,0:T(8,128)S(1)} %next_message.4.mine_ref.own_ref, ...), custom_call_target="tpu_custom_call", output_to_operand_aliasing={{0}: (10, {}), {1}: (11, {})} | custom-call | flops 134217728 | bytes 4194304 | tf_op jit(solution)/shard_map/finish/pallas_call | solution.py:334
  (34 shorter events, 2.7 us)
Async XLA Ops:
  0.6 5.4 %copy-start.11 = (s32[512]{0:T(512)S(1)}, s32[512]{0:T(512)}, u32[]{:S(2)}) copy-start(s32[512]{0:T(512)} %param.12) | copy-start | bytes 6148
  3.0 14.3 %collective-permute-start.3 = (f32[520,128]{1,0:T(8,128)}, f32[520,128]{1,0:T(8,128)S(1)}, u32[]{:S(2)}, u32[]{:S(2)}) collective-permute-start(f32[520,128]{1,0:T(8,128)} %get-tuple-element.17.mine_ref.own_ref), channel_id=1, source_target_pairs={{0,2},{2,0},{4,6},{6,4},{8,10},{10,8},{12,14},{14,12},{1,3},{3,1},... | collective-permute-start | bytes 798728 | tf_op jit(solution)/shard_map/ppermute | solution.py:378
  6.0 1.6 %copy-start.1 = (bf16[512,2048]{1,0:T(8,128)(2,1)S(1)}, bf16[512,2048]{1,0:T(8,128)(2,1)}, u32[]{:S(2)}) copy-start(bf16[512,2048]{1,0:T(8,128)(2,1)} %k_hbm.15) | copy-start | bytes 6291460
  7.6 1.6 %copy-start.3 = (bf16[512,2048]{1,0:T(8,128)(2,1)S(1)}, bf16[512,2048]{1,0:T(8,128)(2,1)}, u32[]{:S(2)}) copy-start(bf16[512,2048]{1,0:T(8,128)(2,1)} %v_hbm.15) | copy-start | bytes 6291460
  9.2 0.8 %copy-start.6 = (f32[16,512]{1,0:T(8,128)S(1)}, f32[16,512]{1,0:T(8,128)}, u32[]{:S(2)}) copy-start(f32[16,512]{1,0:T(8,128)} %get-tuple-element.15.a_ref) | copy-start | bytes 98308
  10.0 0.8 %copy-start.9 = (f32[16,512]{1,0:T(8,128)S(1)}, f32[16,512]{1,0:T(8,128)}, u32[]{:S(2)}) copy-start(f32[16,512]{1,0:T(8,128)} %get-tuple-element.16.w_ref.gate_ref) | copy-start | bytes 98308
  10.7 1.6 %copy-start = (bf16[512,2048]{1,0:T(8,128)(2,1)S(1)}, bf16[512,2048]{1,0:T(8,128)(2,1)}, u32[]{:S(2)}) copy-start(bf16[512,2048]{1,0:T(8,128)(2,1)} %q_ref.7) | copy-start | bytes 6291460
  10.7 1.6 %copy-start.7 = (f32[16,512]{1,0:T(8,128)S(1)}, f32[16,512]{1,0:T(8,128)}, u32[]{:S(2)}) copy-start(f32[16,512]{1,0:T(8,128)} %get-tuple-element.15.a_ref) | copy-start | bytes 98308
  11.3 13.2 %collective-permute-start = (f32[520,128]{1,0:T(8,128)S(1)}, f32[520,128]{1,0:T(8,128)S(1)}, u32[]{:S(2)}, u32[]{:S(2)}) collective-permute-start(f32[520,128]{1,0:T(8,128)S(1)} %next_message.3.mine_ref.own_ref), channel_id=1, source_target_pairs={{0,2},{2,0},{4,6},{6,4},{8,10},{10,8},{12,14},{14,12},{1,3},{3,1},... | collective-permute-start | bytes 798728 | tf_op jit(solution)/shard_map/ppermute | solution.py:380
  12.3 1.6 %copy-start.2 = (bf16[512,2048]{1,0:T(8,128)(2,1)S(1)}, bf16[512,2048]{1,0:T(8,128)(2,1)}, u32[]{:S(2)}) copy-start(bf16[512,2048]{1,0:T(8,128)(2,1)} %k_hbm.15) | copy-start | bytes 6291460
  13.9 1.6 %copy-start.4 = (bf16[512,2048]{1,0:T(8,128)(2,1)S(1)}, bf16[512,2048]{1,0:T(8,128)(2,1)}, u32[]{:S(2)}) copy-start(bf16[512,2048]{1,0:T(8,128)(2,1)} %v_hbm.15) | copy-start | bytes 6291460
  15.5 1.9 %copy-start.8 = (f32[520,128]{1,0:T(8,128)S(1)}, f32[520,128]{1,0:T(8,128)}, u32[]{:S(2)}) copy-start(f32[520,128]{1,0:T(8,128)} %get-tuple-element.17.mine_ref.own_ref) | copy-start | bytes 798724
  15.5 5.4 %copy-start.10 = (f32[16,512]{1,0:T(8,128)S(1)}, f32[16,512]{1,0:T(8,128)}, u32[]{:S(2)}) copy-start(f32[16,512]{1,0:T(8,128)} %get-tuple-element.16.w_ref.gate_ref) | copy-start | bytes 98308
  17.4 15.9 %collective-permute-start.4 = (f32[520,128]{1,0:T(8,128)S(1)}, f32[520,128]{1,0:T(8,128)S(1)}, u32[]{:S(2)}, u32[]{:S(2)}) collective-permute-start(f32[520,128]{1,0:T(8,128)S(1)} %join_windows.5.gate_ref), channel_id=1, source_target_pairs={{0,4},{2,6},{4,8},{6,10},{8,12},{10,14},{1,5},{3,7},{5,9},{7,11},{... | collective-permute-start | bytes 798728 | tf_op jit(solution)/shard_map/ppermute | solution.py:385
  21.5 13.7 %collective-permute-start.6 = (f32[520,128]{1,0:T(8,128)S(1)}, f32[520,128]{1,0:T(8,128)S(1)}, u32[]{:S(2)}, u32[]{:S(2)}) collective-permute-start(f32[520,128]{1,0:T(8,128)S(1)} %next_message.5.mine_ref.own_ref), channel_id=1, source_target_pairs={{0,2},{2,0},{4,6},{6,4},{8,10},{10,8},{12,14},{14,12},{1,3},{3,1},... | collective-permute-start | bytes 798728 | tf_op jit(solution)/shard_map/ppermute | solution.py:393
  24.5 14.2 %collective-permute-start.2 = (f32[520,128]{1,0:T(8,128)S(1)}, f32[520,128]{1,0:T(8,128)S(1)}, u32[]{:S(2)}, u32[]{:S(2)}) collective-permute-start(f32[520,128]{1,0:T(8,128)S(1)} %join_windows.4.gate_ref), channel_id=1, source_target_pairs={{0,4},{2,6},{4,8},{6,10},{8,12},{10,14},{1,5},{3,7},{5,9},{7,11},{... | collective-permute-start | bytes 798728 | tf_op jit(solution)/shard_map/ppermute | solution.py:385
  28.5 12.0 %collective-permute-start.1 = (f32[520,128]{1,0:T(8,128)S(1)}, f32[520,128]{1,0:T(8,128)S(1)}, u32[]{:S(2)}, u32[]{:S(2)}) collective-permute-start(f32[520,128]{1,0:T(8,128)S(1)} %next_message.4.mine_ref.own_ref), channel_id=1, source_target_pairs={{0,2},{2,0},{4,6},{6,4},{8,10},{10,8},{12,14},{14,12},{1,3},{3,1},... | collective-permute-start | bytes 798728 | tf_op jit(solution)/shard_map/ppermute | solution.py:393
  31.5 1.9 %copy-start.5 = (bf16[512,2048]{1,0:T(8,128)(2,1)S(1)}, bf16[512,2048]{1,0:T(8,128)(2,1)}, u32[]{:S(2)}) copy-start(bf16[512,2048]{1,0:T(8,128)(2,1)} %g_ref.7) | copy-start | bytes 6291460
  31.5 1.9 %copy-start.12 = (f32[2048]{0:T(1024)S(1)}, f32[2048]{0:T(1024)}, u32[]{:S(2)}) copy-start(f32[2048]{0:T(1024)} %param.15) | copy-start | bytes 24580
  35.3 9.5 %collective-permute-start.7 = (f32[520,128]{1,0:T(8,128)S(1)}, f32[520,128]{1,0:T(8,128)S(1)}, u32[]{:S(2)}, u32[]{:S(2)}) collective-permute-start(f32[520,128]{1,0:T(8,128)S(1)} %join_windows.7), channel_id=1, source_target_pairs={{0,4},{2,6},{4,8},{6,10},{8,12},{10,14},{1,5},{3,7},{5,9},{7,11},{... | collective-permute-start | bytes 798728 | tf_op jit(solution)/shard_map/ppermute | solution.py:385
  40.6 8.0 %collective-permute-start.5 = (f32[520,128]{1,0:T(8,128)S(1)}, f32[520,128]{1,0:T(8,128)S(1)}, u32[]{:S(2)}, u32[]{:S(2)}) collective-permute-start(f32[520,128]{1,0:T(8,128)S(1)} %join_windows.6), channel_id=1, source_target_pairs={{0,4},{2,6},{4,8},{6,10},{8,12},{10,14},{1,5},{3,7},{5,9},{7,11},{... | collective-permute-start | bytes 798728 | tf_op jit(solution)/shard_map/ppermute | solution.py:385
where the time goes:
time: 50.9 us; the launch traced here: 50.4 us
  Pallas kernels  18.7 us (37%)
  starting transfers between devices  17.6 us (35%)
  local copies, waits for them, and re-layouts  8.88 us (17%)
  waiting for transfers between devices  4.36 us (9%)
  between operations  0.85 us (2%)
    ppermute x4, starting transfers between devices, shards(): lax.ppermute(both[i], 'seq', [(c, c + 2) for c in range(count - 2)])  12.4 us
    unnamed x26, local copies, waits for them, and re-layouts  8.88 us
    pallas_call x4, Pallas kernels, intra(): pl.pallas_call(functools.partial(intra_kernel, first, heads), in_specs=[p...  7.39 us
    pallas_call x4, Pallas kernels, finish(): pl.pallas_call(functools.partial(final_kernel, first, heads), grid=(1,),...  7.17 us
    ppermute x4, waiting for transfers between devices, shards(): lax.ppermute(both[i], 'seq', [(c, c + 2) for c in range(count - 2)])  4.35 us
    ppermute x1, starting transfers between devices, shards(): pair[0] = lax.ppermute(own[0], 'seq', swap)  3 us
    pallas_call x1, Pallas kernels, first_message(): pl.pallas_call(functools.partial(first_kernel, heads, chunk), in_specs=[p...  2.39 us
    ppermute x2, starting transfers between devices, shards(): pair[i + 2] = lax.ppermute(own[i + 2], 'seq', swap)  2.18 us
  transfers between devices with their start and end apart: 8, of which 2 were waited for; matrix products, arithmetic and copies ran while one was open for 0% of the time, Pallas kernels for 29%

commit v1 on v0

--- a/solution.py
+++ b/solution.py
@@ -12,7 +12,6 @@
 NN = (((1,), (0,)), ((), ()))
 NT = (((1,), (1,)), ((), ()))
 MIB = 1 << 20
-FIRST_LIMIT = 62 * MIB
 
 
 def vmem_spec(shape, index_map):
@@ -109,21 +108,21 @@
     return pl.pallas_call(
         functools.partial(first_kernel, heads, chunk),
         in_specs=[pl.BlockSpec(memory_space=pltpu.HBM)] * 5,
-        out_specs=[pl.BlockSpec(memory_space=pltpu.VMEM)] * 3,
+        out_specs=[pl.BlockSpec(memory_space=pltpu.VMEM)] * 4,
         out_shape=[
-            jax.ShapeDtypeStruct((rows, size), F32),
-            jax.ShapeDtypeStruct((heads, tokens), F32),
-            jax.ShapeDtypeStruct((heads, tokens), F32),
+            pltpu.VMEM((rows, size), F32),
+            pltpu.VMEM((heads, tokens), F32),
+            pltpu.VMEM((heads, tokens), F32),
+            pltpu.VMEM((1, tokens), jnp.int32),
         ],
         scratch_shapes=[
-            pltpu.VMEM((1, tokens), jnp.int32),
             pltpu.VMEM((1, heads), jnp.int32),
             pltpu.VMEM((heads, tokens), F32),
             pltpu.VMEM((tokens, chunk * size), BF16),
             pltpu.VMEM((tokens, chunk * size), BF16),
             pltpu.SemaphoreType.DMA((5,)),
         ],
-        compiler_params=pltpu.CompilerParams(vmem_limit_bytes=FIRST_LIMIT),
+        compiler_params=pltpu.CompilerParams(vmem_limit_bytes=16 * MIB),
         cost_estimate=pl.CostEstimate(
             flops=2 * tokens * chunk * size * size, bytes_accessed=2 * MIB, transcendentals=0
         ),
@@ -157,7 +156,7 @@
         + [pl.BlockSpec(memory_space=pltpu.VMEM)] * 3
         + [pl.BlockSpec(memory_space=pl.ANY)],
         out_specs=pl.BlockSpec(memory_space=pltpu.VMEM),
-        out_shape=jax.ShapeDtypeStruct((rows, size), F32),
+        out_shape=pltpu.VMEM((rows, size), F32),
         scratch_shapes=[
             pltpu.VMEM((tokens, heads * size), BF16),
             pltpu.VMEM((tokens, heads * size), BF16),
@@ -199,7 +198,7 @@
         + [pl.BlockSpec(memory_space=pltpu.VMEM)] * 2
         + [pl.BlockSpec(memory_space=pl.ANY)] * len(after),
         out_specs=pl.BlockSpec(memory_space=pltpu.VMEM),
-        out_shape=jax.ShapeDtypeStruct((rows, size), F32),
+        out_shape=pltpu.VMEM((rows, size), F32),
         compiler_params=pltpu.CompilerParams(vmem_limit_bytes=16 * MIB),
         cost_estimate=pl.CostEstimate(
             flops=3 * rows * size, bytes_accessed=12 * rows * size, transcendentals=0
@@ -259,7 +258,7 @@
         in_specs=[pl.BlockSpec(memory_space=pltpu.VMEM)] * 2
         + [pl.BlockSpec(memory_space=pltpu.HBM)] * 3,
         out_specs=pl.BlockSpec(memory_space=pltpu.VMEM),
-        out_shape=jax.ShapeDtypeStruct((tokens, heads * size), F32),
+        out_shape=pltpu.VMEM((tokens, heads * size), F32),
         scratch_shapes=[pltpu.VMEM((tokens, tokens), F32)]
         + [pltpu.VMEM((tokens, heads * size), BF16)] * 3
         + [pltpu.SemaphoreType.DMA((3,))],
@@ -369,32 +368,48 @@
     firsts = list(range(0, heads, chunk))
     seg = segment.reshape(1, tokens)
     gain = norm_gain.reshape(1, -1)
+    far = lambda x: pltpu.with_memory_space_constraint(x, pltpu.HBM)
+    q_far, k, v, seg, retention = far(q), far(k), far(v), far(seg), far(retention)
+    exponent = far(decay_exponent.reshape(1, heads))
     order = lax.rem(place, 2).astype(jnp.int32).reshape(1)
     swap = [(c, c ^ 1) for c in range(count)]
 
-    own, pair, both, before, o = {}, {}, {}, {}, {}
-    tokens_of, so_far = {}, ()
-    own[0], a, w = first_message(seg, decay_exponent.reshape(1, heads), retention, k, v, heads, chunk)
-    pair[0] = lax.ppermute(own[0], "seq", swap)
-    own[1] = next_message(k, v, seg, a, w, w, firsts[1], chunk)
-    pair[1] = lax.ppermute(own[1], "seq", swap)
-    for i, first in enumerate(firsts):
-        o[i] = intra(seg, a, q, k, v, first, chunk)
-        after = (o[i],) + ((tokens_of[i - 2],) if i > 1 else ())
+    own, pair, both, before, o, done = {}, {}, {}, {}, {}, {}
+    result = ()
+    last = len(firsts) - 1
+
+    def exchange(i):
+        pair[i] = lax.ppermute(own[i], "seq", swap)
+
+    def inside(i):
+        o[i] = intra(seg, a, q_far, k, v, firsts[i], chunk)
+
+    def pass_on(i, after):
         both[i] = joined(order, own[i], pair[i], chunk, after)
         before[i] = lax.ppermute(both[i], "seq", [(c, c + 2) for c in range(count - 2)])
         window = 2
         while window < reach:
-            far = lax.ppermute(before[i], "seq", [(c, c + window) for c in range(count - window)])
-            before[i] = joined(jnp.ones((1,), jnp.int32), before[i], far, chunk)
+            past = lax.ppermute(before[i], "seq", [(c, c + window) for c in range(count - window)])
+            before[i] = joined(jnp.ones((1,), jnp.int32), before[i], past, chunk)
             window *= 2
-        if i + 2 < len(firsts):
+
+    own[0], a, w, seg = first_message(seg, exponent, retention, k, v, heads, chunk)
+    exchange(0)
+    own[1] = next_message(k, v, seg, a, w, w, firsts[1], chunk)
+    exchange(1)
+    inside(0)
+    for i, first in enumerate(firsts):
+        if i < last:
+            inside(i + 1)
+        pass_on(i, (o[0], o[min(i + 1, last)]) + ((done[0],) if i == last else ()))
+        if i + 2 <= last:
             own[i + 2] = next_message(k, v, seg, a, w, both[i], firsts[i + 2], chunk)
-            pair[i + 2] = lax.ppermute(own[i + 2], "seq", swap)
-        *so_far, tokens_of[i] = finish(
-            order, seg, a, own[i], pair[i], before[i], o[i], gain, q, g, so_far, first, chunk
-        )
-    return tuple(so_far)
+            exchange(i + 2)
+        for j in {last - 1: (0,), last: range(1, last + 1)}.get(i, ()):
+            *result, done[j] = finish(
+                order, seg, a, own[j], pair[j], before[j], o[j], gain, q, g, result, firsts[j], chunk
+            )
+    return tuple(result)
 
 
 def solution(mesh):

time: 50.9 us -> 47.1 us (0.925)
  local copies, waits for them, and re-layouts: 8.88 us -> 0.02 us
  Pallas kernels: 18.7 us -> 25.3 us
  waiting for transfers between devices: 4.36 us -> 2.09 us
  starting transfers between devices: 17.6 us -> 18.4 us
    unnamed x26 -> x6, local copies, waits for them, and re-layouts: 8.88 us -> 0.02 us
    pallas_call x4, Pallas kernels: 7.39 us -> 11.5 us  [intra(): pl.pallas_call(functools.partial(intra_kernel, first, heads), in_specs=[p...]
    pallas_call x3, Pallas kernels: 1.56 us -> 4.75 us  [next_message(): pl.pallas_call(functools.partial(next_kernel, first, heads), in_specs=[pl...]
    ppermute x8, waiting for transfers between devices: 4.36 us -> 2.09 us  [the longest x4 2.08 us: pass_on(): lax.ppermute(both[i], 'seq', [(c, c + 2) for c in range(count - 2)])]
    ppermute x8, starting transfers between devices: 17.6 us -> 18.4 us  [the longest x4 13.2 us: pass_on(): lax.ppermute(both[i], 'seq', [(c, c + 2) for c in range(count - 2)])]
    pallas_call x1, Pallas kernels: 2.39 us -> 1.67 us  [first_message(): pl.pallas_call(functools.partial(first_kernel, heads, chunk), in_specs=[p...]
  transfers between devices with their start and end apart: 8 -> 8, of which waited for: 2 -> 1; matrix products, arithmetic and copies ran while one was open for 0% -> 0% of each run, Pallas kernels for 29% -> 47%
where the time goes in v1:
time: 47.1 us; the launch traced here: 46.7 us
  Pallas kernels  25.3 us (54%)
  starting transfers between devices  18.4 us (39%)
  waiting for transfers between devices  2.09 us (4%)
  between operations  0.85 us (2%)
    ppermute x4, starting transfers between devices, pass_on(): lax.ppermute(both[i], 'seq', [(c, c + 2) for c in range(count - 2)])  13.2 us
    pallas_call x4, Pallas kernels, intra(): pl.pallas_call(functools.partial(intra_kernel, first, heads), in_specs=[p...  11.5 us
    pallas_call x4, Pallas kernels, finish(): pl.pallas_call(functools.partial(final_kernel, first, heads), grid=(1,),...  7.16 us
    ppermute x4, starting transfers between devices, exchange(): pair[i] = lax.ppermute(own[i], 'seq', swap)  5.24 us
    pallas_call x3, Pallas kernels, next_message(): pl.pallas_call(functools.partial(next_kernel, first, heads), in_specs=[pl...  4.75 us
    ppermute x4, waiting for transfers between devices, pass_on(): lax.ppermute(both[i], 'seq', [(c, c + 2) for c in range(count - 2)])  2.08 us
    pallas_call x1, Pallas kernels, first_message(): pl.pallas_call(functools.partial(first_kernel, heads, chunk), in_specs=[p...  1.67 us
  transfers between devices with their start and end apart: 8, of which 1 were waited for; matrix products, arithmetic and copies ran while one was open for 0% of the time, Pallas kernels for 47%

profile of v1, /device:TPU:0, one launch (start us, length us, event | category | flops | bytes accessed | tf_op | source)
XLA Modules:
  0.0 46.7 jit_solution(5943420029461288384)
XLA Ops:
  0.6 1.7 %first_message.1 = (f32[520,128]{1,0:T(8,128)S(1)}, f32[16,512]{1,0:T(8,128)S(1)}, f32[16,512]{1,0:T(8,128)S(1)}, s32[1,512]{1,0:T(1,128)S(1)}) custom-call(s32[1,512]{1,0:T(1,128)} %bitcast.8, s32[1,16]{1,0:T(1,128)} %bitcast.9, f32[16,512]{1,0:T(8,128)} %keep_hbm.1, bf16[512,2048]{1,0:T(8,128)(2,1)} %k_hbm.15, bf16[512,2048]{1,0:T(8,128)(2,1)} %v_hbm.15), custom_call_target="tpu_custom_call" | custom-call | flops 67108864 | bytes 2097152 | tf_op jit(solution)/shard_map/first_message/pallas_call | solution.py:108
  2.3 3.0 %collective-permute-start.2 = (f32[520,128]{1,0:T(8,128)S(1)}, f32[520,128]{1,0:T(8,128)S(1)}, u32[]{:S(2)}, u32[]{:S(2)}) collective-permute-start(f32[520,128]{1,0:T(8,128)S(1)} %get-tuple-element.18.mine_ref.own_ref), channel_id=1, source_target_pairs={{0,2},{2,0},{4,6},{6,4},{8,10},{10,8},{12,14},{14,12},{1,3},{3,1},... | collective-permute-start | bytes 798728 | tf_op jit(solution)/shard_map/ppermute | solution.py:382
  5.3 1.6 %next_message.3.mine_ref.own_ref = f32[520,128]{1,0:T(8,128)S(1)} custom-call(bf16[512,2048]{1,0:T(8,128)(2,1)} %k_hbm.15, bf16[512,2048]{1,0:T(8,128)(2,1)} %v_hbm.15, s32[1,512]{1,0:T(1,128)S(1)} %get-tuple-element.15.seg_ref, f32[16,512]{1,0:T(8,128)S(1)} %get-tuple-element.16.a_ref, f32[16,512]{1,0:T(8,128)S(1)} %get-tuple-element.17.w_ref.gate_ref, ...), custom_call_target="tpu_custom_call" | custom-call | flops 67108864 | bytes 2097152 | tf_op jit(solution)/shard_map/next_message/pallas_call | solution.py:153
  6.9 0.1 collective-permute-start
  7.0 2.8 %intra_span.4.rest_0_.o_ref = f32[512,512]{1,0:T(8,128)S(1)} custom-call(s32[1,512]{1,0:T(1,128)S(1)} %get-tuple-element.15.seg_ref, f32[16,512]{1,0:T(8,128)S(1)} %get-tuple-element.16.a_ref, bf16[512,2048]{1,0:T(8,128)(2,1)} %q_ref.7, bf16[512,2048]{1,0:T(8,128)(2,1)} %k_hbm.15, bf16[512,2048]{1,0:T(8,128)(2,1)} %v_hbm.15), custom_call_target="tpu_custom_call" | custom-call | flops 402653184 | bytes 3145728 | tf_op jit(solution)/shard_map/intra_span/pallas_call | solution.py:256
  9.9 2.9 %intra_span.7.rest_1_.o_ref = f32[512,512]{1,0:T(8,128)S(1)} custom-call(s32[1,512]{1,0:T(1,128)S(1)} %get-tuple-element.15.seg_ref, f32[16,512]{1,0:T(8,128)S(1)} %get-tuple-element.16.a_ref, bf16[512,2048]{1,0:T(8,128)(2,1)} %q_ref.7, bf16[512,2048]{1,0:T(8,128)(2,1)} %k_hbm.15, bf16[512,2048]{1,0:T(8,128)(2,1)} %v_hbm.15), custom_call_target="tpu_custom_call" | custom-call | flops 402653184 | bytes 3145728 | tf_op jit(solution)/shard_map/intra_span/pallas_call | solution.py:256
  12.7 0.1 join_windows.5.gate_ref
  12.8 4.0 %collective-permute-start.3 = (f32[520,128]{1,0:T(8,128)S(1)}, f32[520,128]{1,0:T(8,128)S(1)}, u32[]{:S(2)}, u32[]{:S(2)}) collective-permute-start(f32[520,128]{1,0:T(8,128)S(1)} %join_windows.5.gate_ref), channel_id=1, source_target_pairs={{0,4},{2,6},{4,8},{6,10},{8,12},{10,14},{1,5},{3,7},{5,9},{7,11},{... | collective-permute-start | bytes 798728 | tf_op jit(solution)/shard_map/ppermute | solution.py:389
  16.8 1.6 %next_message.5.mine_ref.own_ref = f32[520,128]{1,0:T(8,128)S(1)} custom-call(bf16[512,2048]{1,0:T(8,128)(2,1)} %k_hbm.15, bf16[512,2048]{1,0:T(8,128)(2,1)} %v_hbm.15, s32[1,512]{1,0:T(1,128)S(1)} %get-tuple-element.15.seg_ref, f32[16,512]{1,0:T(8,128)S(1)} %get-tuple-element.16.a_ref, f32[16,512]{1,0:T(8,128)S(1)} %get-tuple-element.17.w_ref.gate_ref, ...), custom_call_target="tpu_custom_call" | custom-call | flops 67108864 | bytes 2097152 | tf_op jit(solution)/shard_map/next_message/pallas_call | solution.py:153
  18.4 1.6 %collective-permute-start.5 = (f32[520,128]{1,0:T(8,128)S(1)}, f32[520,128]{1,0:T(8,128)S(1)}, u32[]{:S(2)}, u32[]{:S(2)}) collective-permute-start(f32[520,128]{1,0:T(8,128)S(1)} %next_message.5.mine_ref.own_ref), channel_id=1, source_target_pairs={{0,2},{2,0},{4,6},{6,4},{8,10},{10,8},{12,14},{14,12},{1,3},{3,1},... | collective-permute-start | bytes 798728 | tf_op jit(solution)/shard_map/ppermute | solution.py:382
  19.9 2.8 %intra_span.5.rest_1_.o_ref = f32[512,512]{1,0:T(8,128)S(1)} custom-call(s32[1,512]{1,0:T(1,128)S(1)} %get-tuple-element.15.seg_ref, f32[16,512]{1,0:T(8,128)S(1)} %get-tuple-element.16.a_ref, bf16[512,2048]{1,0:T(8,128)(2,1)} %q_ref.7, bf16[512,2048]{1,0:T(8,128)(2,1)} %k_hbm.15, bf16[512,2048]{1,0:T(8,128)(2,1)} %v_hbm.15), custom_call_target="tpu_custom_call" | custom-call | flops 402653184 | bytes 3145728 | tf_op jit(solution)/shard_map/intra_span/pallas_call | solution.py:256
  22.8 1.6 %next_message.4.mine_ref.own_ref = f32[520,128]{1,0:T(8,128)S(1)} custom-call(bf16[512,2048]{1,0:T(8,128)(2,1)} %k_hbm.15, bf16[512,2048]{1,0:T(8,128)(2,1)} %v_hbm.15, s32[1,512]{1,0:T(1,128)S(1)} %get-tuple-element.15.seg_ref, f32[16,512]{1,0:T(8,128)S(1)} %get-tuple-element.16.a_ref, f32[16,512]{1,0:T(8,128)S(1)} %get-tuple-element.17.w_ref.gate_ref, ...), custom_call_target="tpu_custom_call" | custom-call | flops 67108864 | bytes 2097152 | tf_op jit(solution)/shard_map/next_message/pallas_call | solution.py:153
  24.4 0.6 %collective-permute-start.1 = (f32[520,128]{1,0:T(8,128)S(1)}, f32[520,128]{1,0:T(8,128)S(1)}, u32[]{:S(2)}, u32[]{:S(2)}) collective-permute-start(f32[520,128]{1,0:T(8,128)S(1)} %next_message.4.mine_ref.own_ref), channel_id=1, source_target_pairs={{0,2},{2,0},{4,6},{6,4},{8,10},{10,8},{12,14},{14,12},{1,3},{3,1},... | collective-permute-start | bytes 798728 | tf_op jit(solution)/shard_map/ppermute | solution.py:382
  25.0 3.5 %collective-permute-start.7 = (f32[520,128]{1,0:T(8,128)S(1)}, f32[520,128]{1,0:T(8,128)S(1)}, u32[]{:S(2)}, u32[]{:S(2)}) collective-permute-start(f32[520,128]{1,0:T(8,128)S(1)} %join_windows.4.gate_ref), channel_id=1, source_target_pairs={{0,4},{2,6},{4,8},{6,10},{8,12},{10,14},{1,5},{3,7},{5,9},{7,11},{... | collective-permute-start | bytes 798728 | tf_op jit(solution)/shard_map/ppermute | solution.py:389
  28.5 3.0 %intra_span.6.rest_1_.o_ref = f32[512,512]{1,0:T(8,128)S(1)} custom-call(s32[1,512]{1,0:T(1,128)S(1)} %get-tuple-element.15.seg_ref, f32[16,512]{1,0:T(8,128)S(1)} %get-tuple-element.16.a_ref, bf16[512,2048]{1,0:T(8,128)(2,1)} %q_ref.7, bf16[512,2048]{1,0:T(8,128)(2,1)} %k_hbm.15, bf16[512,2048]{1,0:T(8,128)(2,1)} %v_hbm.15), custom_call_target="tpu_custom_call" | custom-call | flops 402653184 | bytes 3145728 | tf_op jit(solution)/shard_map/intra_span/pallas_call | solution.py:256
  31.6 0.1 join_windows.7
  31.6 3.6 %collective-permute-start.6 = (f32[520,128]{1,0:T(8,128)S(1)}, f32[520,128]{1,0:T(8,128)S(1)}, u32[]{:S(2)}, u32[]{:S(2)}) collective-permute-start(f32[520,128]{1,0:T(8,128)S(1)} %join_windows.7), channel_id=1, source_target_pairs={{0,4},{2,6},{4,8},{6,10},{8,12},{10,14},{1,5},{3,7},{5,9},{7,11},{... | collective-permute-start | bytes 798728 | tf_op jit(solution)/shard_map/ppermute | solution.py:389
  35.3 1.8 %finish.4 = (bf16[512,2048]{1,0:T(8,128)(2,1)}, f32[1,16,128,128]{3,2,1,0:T(8,128)}, f32[8,128]{1,0:T(8,128)S(1)}) custom-call(s32[1]{0:T(128)} %bitcast.order_ref, s32[1,512]{1,0:T(1,128)S(1)} %get-tuple-element.15.seg_ref, f32[16,512]{1,0:T(8,128)S(1)} %get-tuple-element.16.a_ref, f32[520,128]{1,0:T(8,128)S(1)} %get-tuple-element.18.mine_ref.own_ref, ...), custom_call_target="tpu_custom_call" | custom-call | flops 134217728 | bytes 4194304 | tf_op jit(solution)/shard_map/finish/pallas_call | solution.py:333
  37.2 2.1 %collective-permute-start.4 = (f32[520,128]{1,0:T(8,128)S(1)}, f32[520,128]{1,0:T(8,128)S(1)}, u32[]{:S(2)}, u32[]{:S(2)}) collective-permute-start(f32[520,128]{1,0:T(8,128)S(1)} %join_windows.6), channel_id=1, source_target_pairs={{0,4},{2,6},{4,8},{6,10},{8,12},{10,14},{1,5},{3,7},{5,9},{7,11},{... | collective-permute-start | bytes 798728 | tf_op jit(solution)/shard_map/ppermute | solution.py:389
  39.3 1.8 %finish.5 = (bf16[512,2048]{1,0:T(8,128)(2,1)}, f32[1,16,128,128]{3,2,1,0:T(8,128)}, f32[8,128]{1,0:T(8,128)}) custom-call(s32[1]{0:T(128)} %bitcast.order_ref, s32[1,512]{1,0:T(1,128)S(1)} %get-tuple-element.15.seg_ref, f32[16,512]{1,0:T(8,128)S(1)} %get-tuple-element.16.a_ref, ...), custom_call_target="tpu_custom_call", output_to_operand_aliasing={{0}: (10, {}), {1}: (11, {})} | custom-call | flops 134217728 | bytes 4194304 | tf_op jit(solution)/shard_map/finish/pallas_call | solution.py:333
  41.1 0.0 collective-permute-done.6.before_ref
  41.1 1.8 %finish.6 = (bf16[512,2048]{1,0:T(8,128)(2,1)}, f32[1,16,128,128]{3,2,1,0:T(8,128)}, f32[8,128]{1,0:T(8,128)}) custom-call(s32[1]{0:T(128)} %bitcast.order_ref, s32[1,512]{1,0:T(1,128)S(1)} %get-tuple-element.15.seg_ref, f32[16,512]{1,0:T(8,128)S(1)} %get-tuple-element.16.a_ref, ...), custom_call_target="tpu_custom_call", output_to_operand_aliasing={{0}: (10, {}), {1}: (11, {})} | custom-call | flops 134217728 | bytes 4194304 | tf_op jit(solution)/shard_map/finish/pallas_call | solution.py:333
  42.8 2.1 %collective-permute-done.4.before_ref = f32[520,128]{1,0:T(8,128)S(1)} collective-permute-done((f32[520,128]{1,0:T(8,128)S(1)}, f32[520,128]{1,0:T(8,128)S(1)}, u32[]{:S(2)}, u32[]{:S(2)}) %collective-permute-start.4) | collective-permute-done | bytes 266272 | tf_op jit(solution)/shard_map/ppermute | solution.py:389
  44.9 1.8 %finish.7 = (bf16[512,2048]{1,0:T(8,128)(2,1)}, f32[1,16,128,128]{3,2,1,0:T(8,128)}, f32[8,128]{1,0:T(8,128)}) custom-call(s32[1]{0:T(128)} %bitcast.order_ref, s32[1,512]{1,0:T(1,128)S(1)} %get-tuple-element.15.seg_ref, f32[16,512]{1,0:T(8,128)S(1)} %get-tuple-element.16.a_ref, ...), custom_call_target="tpu_custom_call", output_to_operand_aliasing={{0}: (10, {}), {1}: (11, {})} | custom-call | flops 134217728 | bytes 4194304 | tf_op jit(solution)/shard_map/finish/pallas_call | solution.py:333
  (14 shorter events, 0.1 us)
Async XLA Ops:
  2.3 10.4 %collective-permute-start.2 = (f32[520,128]{1,0:T(8,128)S(1)}, f32[520,128]{1,0:T(8,128)S(1)}, u32[]{:S(2)}, u32[]{:S(2)}) collective-permute-start(f32[520,128]{1,0:T(8,128)S(1)} %get-tuple-element.18.mine_ref.own_ref), channel_id=1, source_target_pairs={{0,2},{2,0},{4,6},{6,4},{8,10},{10,8},{12,14},{14,12},{1,3},{3,1},... | collective-permute-start | bytes 798728 | tf_op jit(solution)/shard_map/ppermute | solution.py:382
  6.9 15.9 %collective-permute-start = (f32[520,128]{1,0:T(8,128)S(1)}, f32[520,128]{1,0:T(8,128)S(1)}, u32[]{:S(2)}, u32[]{:S(2)}) collective-permute-start(f32[520,128]{1,0:T(8,128)S(1)} %next_message.3.mine_ref.own_ref), channel_id=1, source_target_pairs={{0,2},{2,0},{4,6},{6,4},{8,10},{10,8},{12,14},{14,12},{1,3},{3,1},... | collective-permute-start | bytes 798728 | tf_op jit(solution)/shard_map/ppermute | solution.py:382
  12.8 22.5 %collective-permute-start.3 = (f32[520,128]{1,0:T(8,128)S(1)}, f32[520,128]{1,0:T(8,128)S(1)}, u32[]{:S(2)}, u32[]{:S(2)}) collective-permute-start(f32[520,128]{1,0:T(8,128)S(1)} %join_windows.5.gate_ref), channel_id=1, source_target_pairs={{0,4},{2,6},{4,8},{6,10},{8,12},{10,14},{1,5},{3,7},{5,9},{7,11},{... | collective-permute-start | bytes 798728 | tf_op jit(solution)/shard_map/ppermute | solution.py:389
  18.4 13.2 %collective-permute-start.5 = (f32[520,128]{1,0:T(8,128)S(1)}, f32[520,128]{1,0:T(8,128)S(1)}, u32[]{:S(2)}, u32[]{:S(2)}) collective-permute-start(f32[520,128]{1,0:T(8,128)S(1)} %next_message.5.mine_ref.own_ref), channel_id=1, source_target_pairs={{0,2},{2,0},{4,6},{6,4},{8,10},{10,8},{12,14},{14,12},{1,3},{3,1},... | collective-permute-start | bytes 798728 | tf_op jit(solution)/shard_map/ppermute | solution.py:382
  24.4 12.7 %collective-permute-start.1 = (f32[520,128]{1,0:T(8,128)S(1)}, f32[520,128]{1,0:T(8,128)S(1)}, u32[]{:S(2)}, u32[]{:S(2)}) collective-permute-start(f32[520,128]{1,0:T(8,128)S(1)} %next_message.4.mine_ref.own_ref), channel_id=1, source_target_pairs={{0,2},{2,0},{4,6},{6,4},{8,10},{10,8},{12,14},{14,12},{1,3},{3,1},... | collective-permute-start | bytes 798728 | tf_op jit(solution)/shard_map/ppermute | solution.py:382
  25.0 14.2 %collective-permute-start.7 = (f32[520,128]{1,0:T(8,128)S(1)}, f32[520,128]{1,0:T(8,128)S(1)}, u32[]{:S(2)}, u32[]{:S(2)}) collective-permute-start(f32[520,128]{1,0:T(8,128)S(1)} %join_windows.4.gate_ref), channel_id=1, source_target_pairs={{0,4},{2,6},{4,8},{6,10},{8,12},{10,14},{1,5},{3,7},{5,9},{7,11},{... | collective-permute-start | bytes 798728 | tf_op jit(solution)/shard_map/ppermute | solution.py:389
  28.5 6.7 %copy-start.1 = (bf16[512,2048]{1,0:T(8,128)(2,1)S(1)}, bf16[512,2048]{1,0:T(8,128)(2,1)}, u32[]{:S(2)}) copy-start(bf16[512,2048]{1,0:T(8,128)(2,1)} %g_ref.7) | copy-start | bytes 6291460
  31.6 3.7 %copy-start = (bf16[512,2048]{1,0:T(8,128)(2,1)S(1)}, bf16[512,2048]{1,0:T(8,128)(2,1)}, u32[]{:S(2)}) copy-start(bf16[512,2048]{1,0:T(8,128)(2,1)} %q_ref.7) | copy-start | bytes 6291460
  31.6 3.7 %copy-start.2 = (f32[2048]{0:T(1024)S(1)}, f32[2048]{0:T(1024)}, u32[]{:S(2)}) copy-start(f32[2048]{0:T(1024)} %param.15) | copy-start | bytes 24580
  31.6 9.4 %collective-permute-start.6 = (f32[520,128]{1,0:T(8,128)S(1)}, f32[520,128]{1,0:T(8,128)S(1)}, u32[]{:S(2)}, u32[]{:S(2)}) collective-permute-start(f32[520,128]{1,0:T(8,128)S(1)} %join_windows.7), channel_id=1, source_target_pairs={{0,4},{2,6},{4,8},{6,10},{8,12},{10,14},{1,5},{3,7},{5,9},{7,11},{... | collective-permute-start | bytes 798728 | tf_op jit(solution)/shard_map/ppermute | solution.py:389
  37.2 7.8 %collective-permute-start.4 = (f32[520,128]{1,0:T(8,128)S(1)}, f32[520,128]{1,0:T(8,128)S(1)}, u32[]{:S(2)}, u32[]{:S(2)}) collective-permute-start(f32[520,128]{1,0:T(8,128)S(1)} %join_windows.6), channel_id=1, source_target_pairs={{0,4},{2,6},{4,8},{6,10},{8,12},{10,14},{1,5},{3,7},{5,9},{7,11},{... | collective-permute-start | bytes 798728 | tf_op jit(solution)/shard_map/ppermute | solution.py:389

commit v2 on v1

v2 whole, which is shorter than its diff:
```python
import functools

import jax
import jax.numpy as jnp
from jax import lax
from jax.experimental import pallas as pl
from jax.experimental.pallas import tpu as pltpu
from jax.sharding import PartitionSpec as P

F32 = jnp.float32
BF16 = jnp.bfloat16
NN = (((1,), (0,)), ((), ()))
NT = (((1,), (1,)), ((), ()))
MIB = 1 << 20


def vmem_spec(shape, index_map):
    return pl.BlockSpec(shape, index_map)


def as_column(row, lanes):
    return jnp.broadcast_to(row, (lanes, row.shape[1])).T


def meta_rows(heads):
    return -(-(heads + 1) // 8) * 8


def put_message(msg_ref, first, heads, size, w_ref, finals, end, k_ref, v_ref):
    top = heads * size
    for j in range(heads):
        columns = slice(j * size, (j + 1) * size)
        weight = w_ref[first + j : first + j + 1, :]
        keyed = (k_ref[:, columns].astype(F32).T * weight).astype(BF16)
        msg_ref[columns, :] = lax.dot_general(
            keyed, v_ref[:, columns], NN, preferred_element_type=F32
        )
    msg_ref[top : top + heads, :] = jnp.broadcast_to(finals, (heads, size))
    below = meta_rows(heads) - heads
    msg_ref[top + heads :, :] = jnp.broadcast_to(end.astype(F32), (below, size))


def first_kernel(
    heads,
    chunk,
    seg_hbm,
    exponent_hbm,
    keep_hbm,
    k_hbm,
    v_hbm,
    msg_ref,
    a_ref,
    w_ref,
    seg_ref,
    k_ref,
    v_ref,
    exponent_ref,
    keep_ref,
    sems,
):
    tokens = seg_ref.shape[1]
    size = msg_ref.shape[1]
    wide = pl.ds(0, chunk * size)
    copies = [
        pltpu.make_async_copy(source, target, sems.at[i])
        for i, (source, target) in enumerate(
            [
                (keep_hbm, keep_ref),
                (exponent_hbm, exponent_ref),
                (seg_hbm, seg_ref),
                (k_hbm.at[:, wide], k_ref),
                (v_hbm.at[:, wide], v_ref),
            ]
        )
    ]
    for copy in copies:
        copy.start()
    earlier = lax.broadcasted_iota(jnp.int32, (tokens, tokens), 0)
    later = lax.broadcasted_iota(jnp.int32, (tokens, tokens), 1)
    upper = jnp.where(earlier <= later, 1.0, 0.0).astype(BF16)
    across = lax.broadcasted_iota(jnp.int32, (heads, heads), 1)
    down = lax.broadcasted_iota(jnp.int32, (heads, heads), 0)
    for copy in copies[:3]:
        copy.wait()
    spread = jnp.broadcast_to(exponent_ref[...], (heads, heads))
    exponent = jnp.sum(jnp.where(across == down, spread, 0).astype(F32), axis=1, keepdims=True)
    a = -jnp.exp2(-exponent) + jnp.log(keep_ref[...])
    high = a.astype(BF16)
    rest = a - high.astype(F32)
    middle = rest.astype(BF16)
    low = (rest - middle.astype(F32)).astype(BF16)
    parts = jnp.concatenate([high, middle, low], axis=0)
    sums = lax.dot_general(parts, upper, NN, preferred_element_type=F32)
    cumulative = sums[:heads] + (sums[heads : 2 * heads] + sums[2 * heads :])
    a_ref[...] = cumulative
    final = cumulative[:, tokens - 1 :]
    seg = seg_ref[...]
    last = seg[:, tokens - 1 :]
    w_ref[...] = jnp.where(seg == last, jnp.exp(final - cumulative), 0.0)
    for copy in copies[3:]:
        copy.wait()
    put_message(msg_ref, 0, chunk, size, w_ref, final[:chunk], last, k_ref, v_ref)


def first_message(seg, exponent, keep, k, v, heads, chunk):
    tokens, size = k.shape[0], k.shape[1] // heads
    rows = chunk * size + meta_rows(chunk)
    return pl.pallas_call(
        functools.partial(first_kernel, heads, chunk),
        in_specs=[pl.BlockSpec(memory_space=pltpu.HBM)] * 5,
        out_specs=[pl.BlockSpec(memory_space=pltpu.VMEM)] * 6,
        out_shape=[
            pltpu.VMEM((rows, size), F32),
            pltpu.VMEM((heads, tokens), F32),
            pltpu.VMEM((heads, tokens), F32),
            pltpu.VMEM((1, tokens), jnp.int32),
            pltpu.VMEM((tokens, chunk * size), BF16),
            pltpu.VMEM((tokens, chunk * size), BF16),
        ],
        scratch_shapes=[
            pltpu.VMEM((1, heads), jnp.int32),
            pltpu.VMEM((heads, tokens), F32),
            pltpu.SemaphoreType.DMA((5,)),
        ],
        compiler_params=pltpu.CompilerParams(vmem_limit_bytes=16 * MIB),
        cost_estimate=pl.CostEstimate(
            flops=2 * tokens * chunk * size * size, bytes_accessed=2 * MIB, transcendentals=0
        ),
        name="first_message",
    )(seg, exponent, keep, k, v)


def prepare_kernel(
    chunk, seg_ref, a_ref, w_ref, q_hbm, k_hbm, v_hbm, mask_ref, *refs
):
    tokens = seg_ref.shape[1]
    heads = a_ref.shape[0]
    count = heads // chunk
    messages, refs = refs[: count - 1], refs[count - 1 :]
    k_refs, refs = refs[: count - 1], refs[count - 1 :]
    v_refs, refs = refs[: count - 1], refs[count - 1 :]
    q_refs, sems = refs[:count], refs[count]
    size = messages[0].shape[1]
    wide = lambda i: pl.ds(i * chunk * size, chunk * size)
    copies = []
    for i in range(1, count):
        for source, target in ((k_hbm, k_refs[i - 1]), (v_hbm, v_refs[i - 1])):
            copies.append((source.at[:, wide(i)], target))
    for i in range(count):
        copies.append((q_hbm.at[:, wide(i)], q_refs[i]))
    copies = [pltpu.make_async_copy(*pair, sems.at[i]) for i, pair in enumerate(copies)]
    for copy in copies:
        copy.start()
    make_mask(seg_ref, mask_ref)
    last = seg_ref[:, tokens - 1 :]
    for i in range(1, count):
        copies[2 * i - 2].wait()
        copies[2 * i - 1].wait()
        first = i * chunk
        final = a_ref[first : first + chunk, tokens - 1 :]
        put_message(
            messages[i - 1], first, chunk, size, w_ref, final, last, k_refs[i - 1], v_refs[i - 1]
        )
    for copy in copies[2 * count - 2 :]:
        copy.wait()


def prepare(seg, a, w, q, k, v, chunk):
    heads = a.shape[0]
    tokens, size = k.shape[0], k.shape[1] // heads
    count = heads // chunk
    rows = chunk * size + meta_rows(chunk)
    near = pltpu.VMEM((tokens, chunk * size), BF16)
    mask, *rest = pl.pallas_call(
        functools.partial(prepare_kernel, chunk),
        in_specs=[pl.BlockSpec(memory_space=pltpu.VMEM)] * 3
        + [pl.BlockSpec(memory_space=pltpu.HBM)] * 3,
        out_specs=[pl.BlockSpec(memory_space=pltpu.VMEM)] * (4 * count - 2),
        out_shape=[pltpu.VMEM((tokens, tokens), F32)]
        + [pltpu.VMEM((rows, size), F32)] * (count - 1)
        + [near] * (3 * count - 2),
        scratch_shapes=[pltpu.SemaphoreType.DMA((3 * count - 2,))],
        compiler_params=pltpu.CompilerParams(vmem_limit_bytes=16 * MIB),
        cost_estimate=pl.CostEstimate(
            flops=2 * tokens * heads * size * size, bytes_accessed=6 * MIB, transcendentals=0
        ),
        name="prepare",
    )(seg, a, w, q, k, v)
    messages, rest = rest[: count - 1], rest[count - 1 :]
    return mask, messages, rest[: count - 1], rest[count - 1 : 2 * count - 2], rest[2 * count - 2 :]


def join_kernel(heads, order_ref, mine_ref, other_ref, *rest):
    out_ref = rest[-1]
    size = mine_ref.shape[1]
    top = heads * size
    mine_later = order_ref[0] == 1
    final_mine, final_other = mine_ref[top : top + heads, :], other_ref[top : top + heads, :]
    end_mine, end_other = mine_ref[top + heads :, :], other_ref[top + heads :, :]
    same = jnp.where(end_mine[:1] == end_other[:1], 1.0, 0.0)
    scale_mine = jnp.where(mine_later, 1.0, jnp.exp(final_other) * same)
    scale_other = jnp.where(mine_later, jnp.exp(final_mine) * same, 1.0)
    for head in range(heads):
        rows = slice(head * size, (head + 1) * size)
        out_ref[rows, :] = (
            scale_mine[head : head + 1] * mine_ref[rows, :]
            + scale_other[head : head + 1] * other_ref[rows, :]
        )
    out_ref[top : top + heads, :] = final_mine + final_other
    out_ref[top + heads :, :] = jnp.where(mine_later, end_mine, end_other)


def joined(order, mine, other, heads, after=(), through=()):
    rows, size = mine.shape
    message = pltpu.VMEM((rows, size), F32)
    vmem, anywhere = pl.BlockSpec(memory_space=pltpu.VMEM), pl.BlockSpec(memory_space=pl.ANY)
    return pl.pallas_call(
        functools.partial(join_kernel, heads),
        in_specs=[pl.BlockSpec(memory_space=pltpu.SMEM), vmem, vmem]
        + [anywhere] * (len(through) + len(after)),
        out_specs=[anywhere] * len(through) + [vmem],
        out_shape=[message] * (len(through) + 1),
        input_output_aliases={3 + i: i for i in range(len(through))},
        compiler_params=pltpu.CompilerParams(vmem_limit_bytes=16 * MIB),
        cost_estimate=pl.CostEstimate(
            flops=3 * rows * size, bytes_accessed=12 * rows * size, transcendentals=0
        ),
        name="join_windows",
    )(order, mine, other, *through, *after)


def make_mask(seg_ref, mask_ref):
    tokens = seg_ref.shape[1]
    seg = seg_ref[...].astype(F32)
    column = as_column(seg, 128)
    for start in range(0, tokens, 128):
        across = lax.broadcasted_iota(jnp.int32, (tokens, 128), 1) + start
        down = lax.broadcasted_iota(jnp.int32, (tokens, 128), 0)
        seen = (column == seg[:, start : start + 128]) & (across <= down)
        mask_ref[:, start : start + 128] = jnp.where(seen, 0.0, -1e30)


def intra_kernel(
    first,
    heads,
    mask_ref,
    a_ref,
    gain_ref,
    q_ref,
    k_ref,
    v_ref,
    g_hbm,
    o_ref,
    decay_ref,
    gate_ref,
    g_ref,
    sems,
):
    tokens = mask_ref.shape[0]
    size = q_ref.shape[1] // heads
    block = min(tokens, 256)
    wide = pl.ds(first * size, heads * size)
    copy = pltpu.make_async_copy(g_hbm.at[:, wide], g_ref, sems.at[0])
    copy.start()
    for j in range(heads):
        columns = slice(j * size, (j + 1) * size)
        a_row = a_ref[first + j : first + j + 1, :] * 1.4426950408889634
        a_column = as_column(a_row, 128)
        decay_ref[:, columns] = jnp.exp2(a_column)
        for start in range(0, tokens, block):
            here, upto = slice(start, start + block), slice(0, start + block)
            scores = lax.dot_general(
                q_ref[here, columns], k_ref[upto, columns], NT, preferred_element_type=F32
            )
            spread = jnp.concatenate([a_column[here]] * ((start + block) // 128), axis=1)
            weight = jnp.exp2(spread - a_row[:, upto] + mask_ref[here, upto])
            probs = (scores * weight).astype(BF16)
            o_ref[here, columns] = lax.dot_general(
                probs, v_ref[upto, columns], NN, preferred_element_type=F32
            )
    copy.wait()
    for j in range(heads):
        columns = slice(j * size, (j + 1) * size)
        half = 0.5 * gain_ref[:, (first + j) * size : (first + j + 1) * size]
        gate_ref[:, columns] = half + half * jnp.tanh(0.5 * g_ref[:, columns].astype(F32))


def intra(mask, a, gain, q, k, v, g, first, heads):
    tokens, size = k.shape[0], k.shape[1] // heads
    vmem = pl.BlockSpec(memory_space=pltpu.VMEM)
    return pl.pallas_call(
        functools.partial(intra_kernel, first, heads),
        in_specs=[vmem] * 6 + [pl.BlockSpec(memory_space=pltpu.HBM)],
        out_specs=[vmem] * 3,
        out_shape=[pltpu.VMEM((tokens, heads * size), F32)] * 3,
        scratch_shapes=[
            pltpu.VMEM((tokens, heads * size), BF16),
            pltpu.SemaphoreType.DMA((1,)),
        ],
        compiler_params=pltpu.CompilerParams(vmem_limit_bytes=16 * MIB),
        cost_estimate=pl.CostEstimate(
            flops=3 * tokens * tokens * heads * size,
            bytes_accessed=3 * MIB,
            transcendentals=tokens * tokens * heads,
        ),
        name="intra_span",
    )(mask, a, gain, q, k, v, g)


def final_kernel(
    first,
    heads,
    order_ref,
    seg_ref,
    own_ref,
    pair_ref,
    before_ref,
    o_ref,
    decay_ref,
    gate_ref,
    q_ref,
    *rest,
):
    gated_hbm, snap_hbm, token_ref, gated_ref, snap_ref, sems = rest[-6:]
    token_ref[...] = jnp.zeros_like(token_ref)
    tokens, size = q_ref.shape[0], own_ref.shape[1]
    top = heads * size
    second = order_ref[0] == 1
    ends = slice(top + heads, top + heads + 1)
    finals = slice(top, top + heads)
    own_end, pair_end, before_end = own_ref[ends, :], pair_ref[ends, :], before_ref[ends, :]
    previous = jnp.where(second, pair_end, before_end)
    kept = jnp.where(own_end == previous, 1.0, 0.0)
    bridged = jnp.where(pair_end == before_end, 1.0, 0.0)
    own_decay = jnp.exp(own_ref[finals, :]) * kept
    from_before = jnp.where(second, jnp.exp(pair_ref[finals, :]) * bridged, 1.0)
    from_pair = jnp.where(second, 1.0, 0.0)
    valid = as_column(jnp.where(seg_ref[...].astype(F32) == previous[:, :1], 1.0, 0.0), size)
    copies = []
    for j in range(heads):
        rows = columns = slice(j * size, (j + 1) * size)
        state = from_before[j : j + 1] * before_ref[rows, :] + from_pair * pair_ref[rows, :]
        snap_ref[j] = own_decay[j : j + 1] * state + own_ref[rows, :]
        high = state.astype(BF16)
        low = (state - high.astype(F32)).astype(BF16)
        q = q_ref[:, columns]
        inter = lax.dot_general(
            jnp.concatenate([q, q], axis=1),
            jnp.concatenate([high, low], axis=0),
            NN,
            preferred_element_type=F32,
        )
        mixed = o_ref[:, columns] + inter * (decay_ref[:, columns] * valid)
        mean_square = jnp.mean(mixed * mixed, axis=1, keepdims=True)
        gated = mixed * lax.rsqrt(mean_square + 1e-06) * gate_ref[:, columns]
        gated_ref[:, columns] = gated.astype(BF16)
        if j % 2 == 1 or j == heads - 1:
            begin = j - j % 2
            width = (j + 1 - begin) * size
            heads_here = pl.ds(first + begin, j + 1 - begin)
            place = pl.ds((first + begin) * size, width)
            for source, target in (
                (gated_ref.at[:, pl.ds(begin * size, width)], gated_hbm.at[:, place]),
                (snap_ref.at[pl.ds(begin, j + 1 - begin)], snap_hbm.at[0, heads_here]),
            ):
                copies.append(pltpu.make_async_copy(source, target, sems.at[len(copies)]))
                copies[-1].start()
    for copy in copies:
        copy.wait()


def finish(order, seg, own, pair, before, o, decay, gate, q, so_far, first, heads, total):
    tokens, size = q.shape[0], q.shape[1] // heads
    vmem, hbm = pl.BlockSpec(memory_space=pltpu.VMEM), pl.BlockSpec(memory_space=pltpu.HBM)
    return pl.pallas_call(
        functools.partial(final_kernel, first, heads),
        in_specs=[pl.BlockSpec(memory_space=pltpu.SMEM)] + [vmem] * 8 + [hbm] * len(so_far),
        out_specs=[hbm, hbm, vmem],
        out_shape=[
            pltpu.HBM((tokens, total * size), BF16),
            pltpu.HBM((1, total, size, size), F32),
            pltpu.VMEM((8, 128), F32),
        ],
        scratch_shapes=[
            pltpu.VMEM((tokens, heads * size), BF16),
            pltpu.VMEM((heads, size, size), F32),
            pltpu.SemaphoreType.DMA((2 * heads,)),
        ],
        input_output_aliases={9 + i: i for i in range(len(so_far))},
        compiler_params=pltpu.CompilerParams(vmem_limit_bytes=16 * MIB),
        cost_estimate=pl.CostEstimate(
            flops=4 * tokens * heads * size * size,
            bytes_accessed=4 * MIB,
            transcendentals=2 * tokens * heads * size,
        ),
        name="finish",
    )(order, seg, own, pair, before, o, decay, gate, q, *so_far)


def shards(q, k, v, g, segment, decay_exponent, retention, norm_gain):
    heads = decay_exponent.shape[0]
    tokens = q.shape[0]
    count = lax.axis_size("seq")
    place = lax.axis_index("seq")
    reach = max(1, count // 4)
    chunk = 4
    firsts = list(range(0, heads, chunk))
    last = len(firsts) - 1
    far = lambda x: pltpu.with_memory_space_constraint(x, pltpu.HBM)
    q, k, v, g = far(q), far(k), far(v), far(g)
    gain = norm_gain.reshape(1, -1)
    order = lax.rem(place, 2).astype(jnp.int32).reshape(1)
    swap = [(c, c ^ 1) for c in range(count)]

    pair, before, inside, done = {}, {}, {}, {}
    result = ()

    own0, a, w, seg, k0, v0 = first_message(
        far(segment.reshape(1, tokens)),
        far(decay_exponent.reshape(1, heads)),
        far(retention),
        k,
        v,
        heads,
        chunk,
    )
    own = [own0]
    pair[0] = lax.ppermute(own[0], "seq", swap)
    mask, messages, k_near, v_near, q_near = prepare(seg, a, w, q, k, v, chunk)
    k_near, v_near = [k0, *k_near], [v0, *v_near]
    own += messages
    pair[1] = lax.ppermute(own[1], "seq", swap)

    def look_inside(i):
        inside[i] = intra(mask, a, gain, q_near[i], k_near[i], v_near[i], g, firsts[i], chunk)

    look_inside(0)
    for i in range(last + 1):
        if i < last:
            look_inside(i + 1)
        after = (inside[0][0], inside[min(i + 1, last)][0]) + ((done[0],) if i == last else ())
        through = (own[i + 2],) if i + 2 <= last else ()
        *through, both = joined(order, own[i], pair[i], chunk, after, through)
        if through:
            own[i + 2] = through[0]
            pair[i + 2] = lax.ppermute(own[i + 2], "seq", swap)
        before[i] = lax.ppermute(both, "seq", [(c, c + 2) for c in range(count - 2)])
        window = 2
        while window < reach:
            past = lax.ppermute(before[i], "seq", [(c, c + window) for c in range(count - window)])
            (before[i],) = joined(jnp.ones((1,), jnp.int32), before[i], past, chunk)
            window *= 2
        for j in {last - 1: (0,), last: range(1, last + 1)}.get(i, ()):
            *result, done[j] = finish(
                order, seg, own[j], pair[j], before[j], *inside[j], q_near[j], result, firsts[j],
                chunk, heads,
            )
    return tuple(result)


def solution(mesh):
    placed = (
        P(("groups", "seq"), "wt"),
        P(("groups", "seq"), "wt"),
        P(("groups", "seq"), "wt"),
        P(("groups", "seq"), "wt"),
        P(("groups", "seq")),
        P("wt"),
        P("wt", ("groups", "seq")),
        P("wt"),
    )
    return jax.shard_map(
        shards,
        mesh=mesh,
        in_specs=placed,
        out_specs=(P(("groups", "seq"), "wt"), P(("groups", "seq"), "wt", None, None)),
        check_vma=False,
    )
```

time: 47.1 us -> 56.1 us (1.19)
  local copies, waits for them, and re-layouts: 0.02 us -> 9.28 us
  waiting for transfers between devices: 2.09 us -> 0.02 us
  Pallas kernels: 25.3 us -> 27.3 us
    unnamed x6 -> x38, local copies, waits for them, and re-layouts: 0.02 us -> 9.28 us
    pallas_call x4, Pallas kernels: 0.19 us -> 2.35 us  [joined(): pl.pallas_call(functools.partial(join_kernel, heads), in_specs=[pl.BlockS...]
    ppermute x8, waiting for transfers between devices: 2.09 us -> 0.02 us  [the longest x4 0.01 us: shards(): lax.ppermute(both, 'seq', [(c, c + 2) for c in range(count - 2)])]
    pallas_call x11 -> x9, Pallas kernels: 23.5 us -> 23.3 us  [the longest x4 10.2 us: intra(): pl.pallas_call(functools.partial(intra_kernel, first, heads), in_specs=[v...]
  transfers between devices with their start and end apart: 8 -> 8, of which waited for: 1 -> 0; matrix products, arithmetic and copies ran while one was open for 0% -> 0% of each run, Pallas kernels for 47% -> 42%
where the time goes in v2:
time: 56.1 us; the launch traced here: 55.5 us
  Pallas kernels  27.3 us (49%)
  starting transfers between devices  18 us (32%)
  local copies, waits for them, and re-layouts  9.28 us (17%)
  between operations  0.91 us (2%)
    ppermute x4, starting transfers between devices, shards(): lax.ppermute(both, 'seq', [(c, c + 2) for c in range(count - 2)])  12.9 us
    pallas_call x4, Pallas kernels, intra(): pl.pallas_call(functools.partial(intra_kernel, first, heads), in_specs=[v...  10.2 us
    pallas_call x4, Pallas kernels, finish(): pl.pallas_call(functools.partial(final_kernel, first, heads), in_specs=[p...  9.82 us
    unnamed x38, local copies, waits for them, and re-layouts  9.28 us
    pallas_call x1, Pallas kernels, prepare(): pl.pallas_call(functools.partial(prepare_kernel, chunk), in_specs=[pl.Blo...  3.34 us
    ppermute x1, starting transfers between devices, shards(): pair[0] = lax.ppermute(own[0], 'seq', swap)  2.94 us
    pallas_call x4, Pallas kernels, joined(): pl.pallas_call(functools.partial(join_kernel, heads), in_specs=[pl.BlockS...  2.35 us
    ppermute x2, starting transfers between devices, shards(): pair[i + 2] = lax.ppermute(own[i + 2], 'seq', swap)  2.16 us
  transfers between devices with their start and end apart: 8, of which 0 were waited for; matrix products, arithmetic and copies ran while one was open for 0% of the time, Pallas kernels for 42%

profile of v2, /device:TPU:0, one launch (start us, length us, event | category | flops | bytes accessed | tf_op | source)
XLA Modules:
  0.0 55.5 jit_solution(10592573587957951203)
XLA Ops:
  0.6 1.7 %first_message.1 = (f32[520,128]{1,0:T(8,128)S(1)}, f32[16,512]{1,0:T(8,128)S(1)}, f32[16,512]{1,0:T(8,128)S(1)}, s32[1,512]{1,0:T(1,128)S(1)}, bf16[512,512]{1,...) custom-call(s32[1,512]{1,0:T(1,128)} %bitcast.8, s32[1,16]{1,0:T(1,128)} %bitcast.9, f32[16,512]{1,0:T(8,128)} %keep_hbm.1, ...), custom_call_target="tpu_custom_call" | custom-call | flops 67108864 | bytes 2097152 | tf_op jit(solution)/shard_map/first_message/pallas_call | solution.py:108
  3.9 2.9 %collective-permute-start.2 = (f32[520,128]{1,0:T(8,128)S(1)}, f32[520,128]{1,0:T(8,128)}, u32[]{:S(2)}, u32[]{:S(2)}) collective-permute-start(f32[520,128]{1,0:T(8,128)S(1)} %get-tuple-element.66.mine_ref.own_ref), channel_id=1, source_target_pairs={{0,2},{2,0},{4,6},{6,4},{8,10},{10,8},{12,14},{14,12},{1,3},{3,1},... | collective-permute-start | bytes 798728 | tf_op jit(solution)/shard_map/ppermute | solution.py:428
  6.8 3.3 %prepare.1 = (f32[512,512]{1,0:T(8,128)S(1)}, f32[520,128]{1,0:T(8,128)}, f32[520,128]{1,0:T(8,128)S(1)}, f32[520,128]{1,0:T(8,128)S(1)}, bf16[512,512]{1,0:T(8,...) custom-call(s32[1,512]{1,0:T(1,128)S(1)} %get-tuple-element.47.seg_r, ...), custom_call_target="tpu_custom_call" | custom-call | flops 268435456 | bytes 6291456 | tf_op jit(solution)/shard_map/prepare/pallas_call | solution.py:174
  11.0 0.8 %copy-done.2 = bf16[512,512]{1,0:T(8,128)(2,1)} copy-done((bf16[512,512]{1,0:T(8,128)(2,1)}, bf16[512,512]{1,0:T(8,128)(2,1)S(1)}, u32[]{:S(2)}) %copy-start.2) | copy-done | bytes 524312
  11.8 0.8 %copy-done.4 = bf16[512,512]{1,0:T(8,128)(2,1)} copy-done((bf16[512,512]{1,0:T(8,128)(2,1)}, bf16[512,512]{1,0:T(8,128)(2,1)S(1)}, u32[]{:S(2)}) %copy-start.4) | copy-done | bytes 524312
  12.6 0.8 %copy-done.6 = bf16[512,512]{1,0:T(8,128)(2,1)} copy-done((bf16[512,512]{1,0:T(8,128)(2,1)}, bf16[512,512]{1,0:T(8,128)(2,1)S(1)}, u32[]{:S(2)}) %copy-start.6) | copy-done | bytes 524312
  13.4 0.8 %copy-done.8 = bf16[512,512]{1,0:T(8,128)(2,1)} copy-done((bf16[512,512]{1,0:T(8,128)(2,1)}, bf16[512,512]{1,0:T(8,128)(2,1)S(1)}, u32[]{:S(2)}) %copy-start.8) | copy-done | bytes 524312
  15.8 1.0 %copy-done.15 = bf16[512,512]{1,0:T(8,128)(2,1)S(1)} copy-done((bf16[512,512]{1,0:T(8,128)(2,1)S(1)}, bf16[512,512]{1,0:T(8,128)(2,1)}, u32[]{:S(2)}) %copy-start.15) | copy-done | bytes 524312
  16.8 1.0 %copy-done.17 = bf16[512,512]{1,0:T(8,128)(2,1)S(1)} copy-done((bf16[512,512]{1,0:T(8,128)(2,1)S(1)}, bf16[512,512]{1,0:T(8,128)(2,1)}, u32[]{:S(2)}) %copy-start.17) | copy-done | bytes 524312
  17.9 2.5 %intra_span.7 = (f32[512,512]{1,0:T(8,128)S(1)}, f32[512,512]{1,0:T(8,128)S(1)}, f32[512,512]{1,0:T(8,128)S(1)}) custom-call(f32[512,512]{1,0:T(8,128)S(1)} %get-tuple-element.52.mask_ref, f32[16,512]{1,0:T(8,128)S(1)} %get-tuple-element.48.a_ref, f32[1,2048]{1,0:T(1,128)S(1)} %bitcast.4, bf16[512,512]{1,0:T(8,128)(2,1)S(1)} %get-tuple-element.68.q_ref, ...), custom_call_target="tpu_custom_call" | custom-call | flops 402653184 | bytes 3145728 | tf_op jit(solution)/shard_map/intra_span/pallas_call | solution.py:291
  20.5 2.5 %intra_span.4 = (f32[512,512]{1,0:T(8,128)S(1)}, f32[512,512]{1,0:T(8,128)S(1)}, f32[512,512]{1,0:T(8,128)S(1)}) custom-call(f32[512,512]{1,0:T(8,128)S(1)} %get-tuple-element.52.mask_ref, f32[16,512]{1,0:T(8,128)S(1)} %get-tuple-element.48.a_ref, f32[1,2048]{1,0:T(1,128)S(1)} %bitcast.5, bf16[512,512]{1,0:T(8,128)(2,1)S(1)} %copy-done.1, ...), custom_call_target="tpu_custom_call" | custom-call | flops 402653184 | bytes 3145728 | tf_op jit(solution)/shard_map/intra_span/pallas_call | solution.py:291
  23.0 1.1 %join_windows.5 = (f32[520,128]{1,0:T(8,128)S(1)}, f32[520,128]{1,0:T(8,128)S(1)}) custom-call(s32[1]{0:T(128)} %bitcast.order_ref, f32[520,128]{1,0:T(8,128)S(1)} %get-tuple-element.66.mine_ref.own_ref, f32[520,128]{1,0:T(8,128)} %collective-permute-done.2.other_ref.pair_ref, ...), custom_call_target="tpu_custom_call", output_to_operand_aliasing={{0}: (3, {})} | custom-call | flops 199680 | bytes 798720 | tf_op jit(solution)/shard_map/join_windows/pallas_call | solution.py:217
  24.1 4.0 %collective-permute-start.3 = (f32[520,128]{1,0:T(8,128)S(1)}, f32[520,128]{1,0:T(8,128)S(1)}, u32[]{:S(2)}, u32[]{:S(2)}) collective-permute-start(f32[520,128]{1,0:T(8,128)S(1)} %get-tuple-element.72), channel_id=1, source_target_pairs={{0,4},{2,6},{4,8},{6,10},{8,12},{10,14},{1,5},{3,7},{5,9},{7,11},{... | collective-permute-start | bytes 798728 | tf_op jit(solution)/shard_map/ppermute | solution.py:447
  28.1 1.6 %collective-permute-start.5 = (f32[520,128]{1,0:T(8,128)S(1)}, f32[520,128]{1,0:T(8,128)S(1)}, u32[]{:S(2)}, u32[]{:S(2)}) collective-permute-start(f32[520,128]{1,0:T(8,128)S(1)} %get-tuple-element.78.mine_ref.own_ref), channel_id=1, source_target_pairs={{0,2},{2,0},{4,6},{6,4},{8,10},{10,8},{12,14},{14,12},{1,3},{3,1},... | collective-permute-start | bytes 798728 | tf_op jit(solution)/shard_map/ppermute | solution.py:446
  29.7 2.5 %intra_span.5 = (f32[512,512]{1,0:T(8,128)S(1)}, f32[512,512]{1,0:T(8,128)S(1)}, f32[512,512]{1,0:T(8,128)S(1)}) custom-call(f32[512,512]{1,0:T(8,128)S(1)} %get-tuple-element.52.mask_ref, f32[16,512]{1,0:T(8,128)S(1)} %get-tuple-element.48.a_ref, f32[1,2048]{1,0:T(1,128)S(1)} %bitcast.6, bf16[512,512]{1,0:T(8,128)(2,1)S(1)} %get-tuple-element.57.q_ref, ...), custom_call_target="tpu_custom_call" | custom-call | flops 402653184 | bytes 3145728 | tf_op jit(solution)/shard_map/intra_span/pallas_call | solution.py:291
  32.3 1.2 %join_windows.4 = (f32[520,128]{1,0:T(8,128)S(1)}, f32[520,128]{1,0:T(8,128)S(1)}) custom-call(s32[1]{0:T(128)} %bitcast.order_ref, f32[520,128]{1,0:T(8,128)} %get-tuple-element.50.mine_ref.own_ref, f32[520,128]{1,0:T(8,128)} %collective-permute-done.other_ref.pair_ref, f32[520,128]{1,0:T(8,128)S(1)} %get-tuple-element.51.rest_0_, ...), custom_call_target="tpu_custom_call", output_to_operand_aliasing={{0}: (3, {})} | custom-call | flops 199680 | bytes 798720 | tf_op jit(solution)/shard_map/join_windows/pallas_call | solution.py:217
  34.0 3.5 %collective-permute-start.7 = (f32[520,128]{1,0:T(8,128)S(1)}, f32[520,128]{1,0:T(8,128)S(1)}, u32[]{:S(2)}, u32[]{:S(2)}) collective-permute-start(f32[520,128]{1,0:T(8,128)S(1)} %get-tuple-element.81), channel_id=1, source_target_pairs={{0,4},{2,6},{4,8},{6,10},{8,12},{10,14},{1,5},{3,7},{5,9},{7,11},{... | collective-permute-start | bytes 798728 | tf_op jit(solution)/shard_map/ppermute | solution.py:447
  37.5 2.6 %intra_span.6 = (f32[512,512]{1,0:T(8,128)S(1)}, f32[512,512]{1,0:T(8,128)S(1)}, f32[512,512]{1,0:T(8,128)S(1)}) custom-call(f32[512,512]{1,0:T(8,128)S(1)} %get-tuple-element.52.mask_ref, f32[16,512]{1,0:T(8,128)S(1)} %get-tuple-element.48.a_ref, f32[1,2048]{1,0:T(1,128)S(1)} %bitcast.7, bf16[512,512]{1,0:T(8,128)(2,1)S(1)} %get-tuple-element.62.q_ref, ...), custom_call_target="tpu_custom_call" | custom-call | flops 402653184 | bytes 3145728 | tf_op jit(solution)/shard_map/intra_span/pallas_call | solution.py:291
  40.2 3.5 %collective-permute-start.6 = (f32[520,128]{1,0:T(8,128)S(1)}, f32[520,128]{1,0:T(8,128)S(1)}, u32[]{:S(2)}, u32[]{:S(2)}) collective-permute-start(f32[520,128]{1,0:T(8,128)S(1)} %join_windows.7), channel_id=1, source_target_pairs={{0,4},{2,6},{4,8},{6,10},{8,12},{10,14},{1,5},{3,7},{5,9},{7,11},{... | collective-permute-start | bytes 798728 | tf_op jit(solution)/shard_map/ppermute | solution.py:447
  43.7 2.5 %finish.4 = (bf16[512,2048]{1,0:T(8,128)(2,1)}, f32[1,16,128,128]{3,2,1,0:T(8,128)}, f32[8,128]{1,0:T(8,128)S(1)}) custom-call(s32[1]{0:T(128)} %bitcast.order_ref, s32[1,512]{1,0:T(1,128)S(1)} %get-tuple-element.47.seg_ref, f32[520,128]{1,0:T(8,128)S(1)} %get-tuple-element.66.mine_ref.own_ref, f32[520,128]{1,0:T(8,128)} %collective-permute-done.2.other_ref.pair_ref, ...), custom_call_target="tpu_custom_call" | custom-call | flops 134217728 | bytes 4194304 | tf_op jit(solution)/shard_map/finish/pallas_call | solution.py:375
  46.2 1.9 %collective-permute-start.4 = (f32[520,128]{1,0:T(8,128)S(1)}, f32[520,128]{1,0:T(8,128)S(1)}, u32[]{:S(2)}, u32[]{:S(2)}) collective-permute-start(f32[520,128]{1,0:T(8,128)S(1)} %join_windows.6), channel_id=1, source_target_pairs={{0,4},{2,6},{4,8},{6,10},{8,12},{10,14},{1,5},{3,7},{5,9},{7,11},{... | collective-permute-start | bytes 798728 | tf_op jit(solution)/shard_map/ppermute | solution.py:447
  48.2 3.1 %finish.5 = (bf16[512,2048]{1,0:T(8,128)(2,1)}, f32[1,16,128,128]{3,2,1,0:T(8,128)}, f32[8,128]{1,0:T(8,128)}) custom-call(s32[1]{0:T(128)} %bitcast.order_ref, s32[1,512]{1,0:T(1,128)S(1)} %get-tuple-element.47.seg_ref, f32[520,128]{1,0:T(8,128)} %get-tuple-element.50.mine_ref.own_ref, ...), custom_call_target="tpu_custom_call", output_to_operand_aliasing={{0}: (9, {}), {1}: (10, {})} | custom-call | flops 134217728 | bytes 4194304 | tf_op jit(solution)/shard_map/finish/pallas_call | solution.py:375
  51.3 2.1 %finish.6 = (bf16[512,2048]{1,0:T(8,128)(2,1)}, f32[1,16,128,128]{3,2,1,0:T(8,128)}, f32[8,128]{1,0:T(8,128)}) custom-call(s32[1]{0:T(128)} %bitcast.order_ref, s32[1,512]{1,0:T(1,128)S(1)} %get-tuple-element.47.seg_ref, f32[520,128]{1,0:T(8,128)S(1)} %get-tuple-element.78.mine_ref.own_ref, ...), custom_call_target="tpu_custom_call", output_to_operand_aliasing={{0}: (9, {}), {1}: (10, {})} | custom-call | flops 134217728 | bytes 4194304 | tf_op jit(solution)/shard_map/finish/pallas_call | solution.py:375
  53.4 2.1 %finish.7 = (bf16[512,2048]{1,0:T(8,128)(2,1)}, f32[1,16,128,128]{3,2,1,0:T(8,128)}, f32[8,128]{1,0:T(8,128)}) custom-call(s32[1]{0:T(128)} %bitcast.order_ref, s32[1,512]{1,0:T(1,128)S(1)} %get-tuple-element.47.seg_ref, f32[520,128]{1,0:T(8,128)S(1)} %get-tuple-element.61.mine_ref.own_ref, ...), custom_call_target="tpu_custom_call", output_to_operand_aliasing={{0}: (9, {}), {1}: (10, {})} | custom-call | flops 134217728 | bytes 4194304 | tf_op jit(solution)/shard_map/finish/pallas_call | solution.py:375
  (44 shorter events, 4.7 us)
Async XLA Ops:
  2.3 0.8 %copy-start.10 = (bf16[512,512]{1,0:T(8,128)(2,1)}, bf16[512,512]{1,0:T(8,128)(2,1)S(1)}, u32[]{:S(2)}) copy-start(bf16[512,512]{1,0:T(8,128)(2,1)S(1)} %get-tuple-element.54.k_ref) | copy-start | bytes 1572868
  3.9 19.1 %collective-permute-start.2 = (f32[520,128]{1,0:T(8,128)S(1)}, f32[520,128]{1,0:T(8,128)}, u32[]{:S(2)}, u32[]{:S(2)}) collective-permute-start(f32[520,128]{1,0:T(8,128)S(1)} %get-tuple-element.66.mine_ref.own_ref), channel_id=1, source_target_pairs={{0,2},{2,0},{4,6},{6,4},{8,10},{10,8},{12,14},{14,12},{1,3},{3,1},... | collective-permute-start | bytes 798728 | tf_op jit(solution)/shard_map/ppermute | solution.py:428
  6.8 9.0 %copy-start.18 = (f32[2048]{0:T(1024)S(1)}, f32[2048]{0:T(1024)}, u32[]{:S(2)}) copy-start(f32[2048]{0:T(1024)} %param.15) | copy-start | bytes 24580
  10.2 0.8 %copy-start = (bf16[512,512]{1,0:T(8,128)(2,1)}, bf16[512,512]{1,0:T(8,128)(2,1)S(1)}, u32[]{:S(2)}) copy-start(bf16[512,512]{1,0:T(8,128)(2,1)S(1)} %get-tuple-element.53.q_ref) | copy-start | bytes 1572868
  11.0 0.8 %copy-start.2 = (bf16[512,512]{1,0:T(8,128)(2,1)}, bf16[512,512]{1,0:T(8,128)(2,1)S(1)}, u32[]{:S(2)}) copy-start(bf16[512,512]{1,0:T(8,128)(2,1)S(1)} %get-tuple-element.63.k_ref) | copy-start | bytes 1572868
  11.8 0.8 %copy-start.4 = (bf16[512,512]{1,0:T(8,128)(2,1)}, bf16[512,512]{1,0:T(8,128)(2,1)S(1)}, u32[]{:S(2)}) copy-start(bf16[512,512]{1,0:T(8,128)(2,1)S(1)} %get-tuple-element.64.v_ref) | copy-start | bytes 1572868
  12.6 0.8 %copy-start.6 = (bf16[512,512]{1,0:T(8,128)(2,1)}, bf16[512,512]{1,0:T(8,128)(2,1)S(1)}, u32[]{:S(2)}) copy-start(bf16[512,512]{1,0:T(8,128)(2,1)S(1)} %get-tuple-element.58.k_ref) | copy-start | bytes 1572868
  13.4 0.8 %copy-start.8 = (bf16[512,512]{1,0:T(8,128)(2,1)}, bf16[512,512]{1,0:T(8,128)(2,1)S(1)}, u32[]{:S(2)}) copy-start(bf16[512,512]{1,0:T(8,128)(2,1)S(1)} %get-tuple-element.59.v_ref) | copy-start | bytes 1572868
  15.8 16.5 %collective-permute-start = (f32[520,128]{1,0:T(8,128)}, f32[520,128]{1,0:T(8,128)}, u32[]{:S(2)}, u32[]{:S(2)}) collective-permute-start(f32[520,128]{1,0:T(8,128)} %get-tuple-element.50.mine_ref.own_ref), channel_id=1, source_target_pairs={{0,2},{2,0},{4,6},{6,4},{8,10},{10,8},{12,14},{14,12},{1,3},{3,1},... | collective-permute-start | bytes 798728 | tf_op jit(solution)/shard_map/ppermute | solution.py:432
  15.8 1.0 %copy-start.15 = (bf16[512,512]{1,0:T(8,128)(2,1)S(1)}, bf16[512,512]{1,0:T(8,128)(2,1)}, u32[]{:S(2)}) copy-start(bf16[512,512]{1,0:T(8,128)(2,1)} %copy-done.14) | copy-start | bytes 1572868
  16.8 1.0 %copy-start.17 = (bf16[512,512]{1,0:T(8,128)(2,1)S(1)}, bf16[512,512]{1,0:T(8,128)(2,1)}, u32[]{:S(2)}) copy-start(bf16[512,512]{1,0:T(8,128)(2,1)} %copy-done.16) | copy-start | bytes 1572868
  17.9 2.5 %copy-start.1 = (bf16[512,512]{1,0:T(8,128)(2,1)S(1)}, bf16[512,512]{1,0:T(8,128)(2,1)}, u32[]{:S(2)}) copy-start(bf16[512,512]{1,0:T(8,128)(2,1)} %copy-done) | copy-start | bytes 1572868
  17.9 2.6 %copy-start.11 = (bf16[512,512]{1,0:T(8,128)(2,1)S(1)}, bf16[512,512]{1,0:T(8,128)(2,1)}, u32[]{:S(2)}) copy-start(bf16[512,512]{1,0:T(8,128)(2,1)} %copy-done.10) | copy-start | bytes 1572868
  17.9 2.6 %copy-start.13 = (bf16[512,512]{1,0:T(8,128)(2,1)S(1)}, bf16[512,512]{1,0:T(8,128)(2,1)}, u32[]{:S(2)}) copy-start(bf16[512,512]{1,0:T(8,128)(2,1)} %copy-done.12) | copy-start | bytes 1572868
  23.0 6.7 %copy-start.7 = (bf16[512,512]{1,0:T(8,128)(2,1)S(1)}, bf16[512,512]{1,0:T(8,128)(2,1)}, u32[]{:S(2)}) copy-start(bf16[512,512]{1,0:T(8,128)(2,1)} %copy-done.6) | copy-start | bytes 1572868
  23.0 6.7 %copy-start.9 = (bf16[512,512]{1,0:T(8,128)(2,1)S(1)}, bf16[512,512]{1,0:T(8,128)(2,1)}, u32[]{:S(2)}) copy-start(bf16[512,512]{1,0:T(8,128)(2,1)} %copy-done.8) | copy-start | bytes 1572868
  24.1 19.6 %collective-permute-start.3 = (f32[520,128]{1,0:T(8,128)S(1)}, f32[520,128]{1,0:T(8,128)S(1)}, u32[]{:S(2)}, u32[]{:S(2)}) collective-permute-start(f32[520,128]{1,0:T(8,128)S(1)} %get-tuple-element.72), channel_id=1, source_target_pairs={{0,4},{2,6},{4,8},{6,10},{8,12},{10,14},{1,5},{3,7},{5,9},{7,11},{... | collective-permute-start | bytes 798728 | tf_op jit(solution)/shard_map/ppermute | solution.py:447
  28.1 12.0 %collective-permute-start.5 = (f32[520,128]{1,0:T(8,128)S(1)}, f32[520,128]{1,0:T(8,128)S(1)}, u32[]{:S(2)}, u32[]{:S(2)}) collective-permute-start(f32[520,128]{1,0:T(8,128)S(1)} %get-tuple-element.78.mine_ref.own_ref), channel_id=1, source_target_pairs={{0,2},{2,0},{4,6},{6,4},{8,10},{10,8},{12,14},{14,12},{1,3},{3,1},... | collective-permute-start | bytes 798728 | tf_op jit(solution)/shard_map/ppermute | solution.py:446
  32.3 5.3 %copy-start.3 = (bf16[512,512]{1,0:T(8,128)(2,1)S(1)}, bf16[512,512]{1,0:T(8,128)(2,1)}, u32[]{:S(2)}) copy-start(bf16[512,512]{1,0:T(8,128)(2,1)} %copy-done.2) | copy-start | bytes 1572868
  32.3 5.3 %copy-start.5 = (bf16[512,512]{1,0:T(8,128)(2,1)S(1)}, bf16[512,512]{1,0:T(8,128)(2,1)}, u32[]{:S(2)}) copy-start(bf16[512,512]{1,0:T(8,128)(2,1)} %copy-done.4) | copy-start | bytes 1572868
  33.4 12.7 %collective-permute-start.1 = (f32[520,128]{1,0:T(8,128)S(1)}, f32[520,128]{1,0:T(8,128)S(1)}, u32[]{:S(2)}, u32[]{:S(2)}) collective-permute-start(f32[520,128]{1,0:T(8,128)S(1)} %get-tuple-element.61.mine_ref.own_ref), channel_id=1, source_target_pairs={{0,2},{2,0},{4,6},{6,4},{8,10},{10,8},{12,14},{14,12},{1,3},{3,1},... | collective-permute-start | bytes 798728 | tf_op jit(solution)/shard_map/ppermute | solution.py:446
  34.0 14.1 %collective-permute-start.7 = (f32[520,128]{1,0:T(8,128)S(1)}, f32[520,128]{1,0:T(8,128)S(1)}, u32[]{:S(2)}, u32[]{:S(2)}) collective-permute-start(f32[520,128]{1,0:T(8,128)S(1)} %get-tuple-element.81), channel_id=1, source_target_pairs={{0,4},{2,6},{4,8},{6,10},{8,12},{10,14},{1,5},{3,7},{5,9},{7,11},{... | collective-permute-start | bytes 798728 | tf_op jit(solution)/shard_map/ppermute | solution.py:447
  40.2 11.1 %collective-permute-start.6 = (f32[520,128]{1,0:T(8,128)S(1)}, f32[520,128]{1,0:T(8,128)S(1)}, u32[]{:S(2)}, u32[]{:S(2)}) collective-permute-start(f32[520,128]{1,0:T(8,128)S(1)} %join_windows.7), channel_id=1, source_target_pairs={{0,4},{2,6},{4,8},{6,10},{8,12},{10,14},{1,5},{3,7},{5,9},{7,11},{... | collective-permute-start | bytes 798728 | tf_op jit(solution)/shard_map/ppermute | solution.py:447
  46.2 7.2 %collective-permute-start.4 = (f32[520,128]{1,0:T(8,128)S(1)}, f32[520,128]{1,0:T(8,128)S(1)}, u32[]{:S(2)}, u32[]{:S(2)}) collective-permute-start(f32[520,128]{1,0:T(8,128)S(1)} %join_windows.6), channel_id=1, source_target_pairs={{0,4},{2,6},{4,8},{6,10},{8,12},{10,14},{1,5},{3,7},{5,9},{7,11},{... | collective-permute-start | bytes 798728 | tf_op jit(solution)/shard_map/ppermute | solution.py:447
  (3 other events, 2.4 us)

commit v3 on v2

--- a/solution.py
+++ b/solution.py
@@ -52,10 +52,10 @@
     a_ref,
     w_ref,
     seg_ref,
+    exponent_ref,
+    keep_ref,
     k_ref,
     v_ref,
-    exponent_ref,
-    keep_ref,
     sems,
 ):
     tokens = seg_ref.shape[1]
@@ -108,21 +108,21 @@
     return pl.pallas_call(
         functools.partial(first_kernel, heads, chunk),
         in_specs=[pl.BlockSpec(memory_space=pltpu.HBM)] * 5,
-        out_specs=[pl.BlockSpec(memory_space=pltpu.VMEM)] * 6,
+        out_specs=[pl.BlockSpec(memory_space=pltpu.VMEM)] * 4,
         out_shape=[
             pltpu.VMEM((rows, size), F32),
             pltpu.VMEM((heads, tokens), F32),
             pltpu.VMEM((heads, tokens), F32),
             pltpu.VMEM((1, tokens), jnp.int32),
-            pltpu.VMEM((tokens, chunk * size), BF16),
-            pltpu.VMEM((tokens, chunk * size), BF16),
         ],
         scratch_shapes=[
             pltpu.VMEM((1, heads), jnp.int32),
             pltpu.VMEM((heads, tokens), F32),
+            pltpu.VMEM((tokens, chunk * size), BF16),
+            pltpu.VMEM((tokens, chunk * size), BF16),
             pltpu.SemaphoreType.DMA((5,)),
         ],
-        compiler_params=pltpu.CompilerParams(vmem_limit_bytes=16 * MIB),
+        compiler_params=pltpu.CompilerParams(vmem_limit_bytes=8 * MIB),
         cost_estimate=pl.CostEstimate(
             flops=2 * tokens * chunk * size * size, bytes_accessed=2 * MIB, transcendentals=0
         ),
@@ -130,71 +130,55 @@
     )(seg, exponent, keep, k, v)
 
 
-def prepare_kernel(
-    chunk, seg_ref, a_ref, w_ref, q_hbm, k_hbm, v_hbm, mask_ref, *refs
-):
-    tokens = seg_ref.shape[1]
-    heads = a_ref.shape[0]
-    count = heads // chunk
-    messages, refs = refs[: count - 1], refs[count - 1 :]
-    k_refs, refs = refs[: count - 1], refs[count - 1 :]
-    v_refs, refs = refs[: count - 1], refs[count - 1 :]
-    q_refs, sems = refs[:count], refs[count]
-    size = messages[0].shape[1]
-    wide = lambda i: pl.ds(i * chunk * size, chunk * size)
+def rest_kernel(chunk, seg_ref, a_ref, w_ref, k_hbm, v_hbm, *refs):
+    messages, (k_ref, v_ref, sems) = refs[:-3], refs[-3:]
+    tokens, size = seg_ref.shape[1], messages[0].shape[1]
     copies = []
-    for i in range(1, count):
-        for source, target in ((k_hbm, k_refs[i - 1]), (v_hbm, v_refs[i - 1])):
-            copies.append((source.at[:, wide(i)], target))
-    for i in range(count):
-        copies.append((q_hbm.at[:, wide(i)], q_refs[i]))
-    copies = [pltpu.make_async_copy(*pair, sems.at[i]) for i, pair in enumerate(copies)]
+    for i in range(len(messages)):
+        wide = pl.ds((i + 1) * chunk * size, chunk * size)
+        copies += [
+            pltpu.make_async_copy(k_hbm.at[:, wide], k_ref.at[i], sems.at[0, i]),
+            pltpu.make_async_copy(v_hbm.at[:, wide], v_ref.at[i], sems.at[1, i]),
+        ]
     for copy in copies:
         copy.start()
-    make_mask(seg_ref, mask_ref)
     last = seg_ref[:, tokens - 1 :]
-    for i in range(1, count):
-        copies[2 * i - 2].wait()
-        copies[2 * i - 1].wait()
-        first = i * chunk
+    for i, msg_ref in enumerate(messages):
+        copies[2 * i].wait()
+        copies[2 * i + 1].wait()
+        first = (i + 1) * chunk
         final = a_ref[first : first + chunk, tokens - 1 :]
-        put_message(
-            messages[i - 1], first, chunk, size, w_ref, final, last, k_refs[i - 1], v_refs[i - 1]
-        )
-    for copy in copies[2 * count - 2 :]:
-        copy.wait()
-
-
-def prepare(seg, a, w, q, k, v, chunk):
+        put_message(msg_ref, first, chunk, size, w_ref, final, last, k_ref.at[i], v_ref.at[i])
+
+
+def rest_messages(seg, a, w, k, v, chunk):
     heads = a.shape[0]
     tokens, size = k.shape[0], k.shape[1] // heads
-    count = heads // chunk
+    count = heads // chunk - 1
     rows = chunk * size + meta_rows(chunk)
-    near = pltpu.VMEM((tokens, chunk * size), BF16)
-    mask, *rest = pl.pallas_call(
-        functools.partial(prepare_kernel, chunk),
+    return pl.pallas_call(
+        functools.partial(rest_kernel, chunk),
         in_specs=[pl.BlockSpec(memory_space=pltpu.VMEM)] * 3
-        + [pl.BlockSpec(memory_space=pltpu.HBM)] * 3,
-        out_specs=[pl.BlockSpec(memory_space=pltpu.VMEM)] * (4 * count - 2),
-        out_shape=[pltpu.VMEM((tokens, tokens), F32)]
-        + [pltpu.VMEM((rows, size), F32)] * (count - 1)
-        + [near] * (3 * count - 2),
-        scratch_shapes=[pltpu.SemaphoreType.DMA((3 * count - 2,))],
-        compiler_params=pltpu.CompilerParams(vmem_limit_bytes=16 * MIB),
+        + [pl.BlockSpec(memory_space=pltpu.HBM)] * 2,
+        out_specs=[pl.BlockSpec(memory_space=pltpu.VMEM)] * count,
+        out_shape=[pltpu.VMEM((rows, size), F32)] * count,
+        scratch_shapes=[pltpu.VMEM((count, tokens, chunk * size), BF16)] * 2
+        + [pltpu.SemaphoreType.DMA((2, count))],
+        compiler_params=pltpu.CompilerParams(vmem_limit_bytes=8 * MIB),
         cost_estimate=pl.CostEstimate(
-            flops=2 * tokens * heads * size * size, bytes_accessed=6 * MIB, transcendentals=0
+            flops=2 * tokens * heads * size * size, bytes_accessed=4 * MIB, transcendentals=0
         ),
-        name="prepare",
-    )(seg, a, w, q, k, v)
-    messages, rest = rest[: count - 1], rest[count - 1 :]
-    return mask, messages, rest[: count - 1], rest[count - 1 : 2 * count - 2], rest[2 * count - 2 :]
+        name="rest_messages",
+    )(seg, a, w, k, v)
 
 
 def join_kernel(heads, order_ref, mine_ref, other_ref, *rest):
-    out_ref = rest[-1]
+    *copied, out_ref = rest
+    if copied:
+        copied[-1][...] = copied[0][...]
     size = mine_ref.shape[1]
     top = heads * size
-    mine_later = order_ref[0] == 1
+    mine_later = (order_ref[0] & 1) == 1
     final_mine, final_other = mine_ref[top : top + heads, :], other_ref[top : top + heads, :]
     end_mine, end_other = mine_ref[top + heads :, :], other_ref[top + heads :, :]
     same = jnp.where(end_mine[:1] == end_other[:1], 1.0, 0.0)
@@ -214,14 +198,19 @@
     rows, size = mine.shape
     message = pltpu.VMEM((rows, size), F32)
     vmem, anywhere = pl.BlockSpec(memory_space=pltpu.VMEM), pl.BlockSpec(memory_space=pl.ANY)
+
+    def kernel(order_ref, mine_ref, other_ref, *rest):
+        rest = rest[: len(through)] + rest[len(through) + len(after) :]
+        join_kernel(heads, order_ref, mine_ref, other_ref, *rest)
+
     return pl.pallas_call(
-        functools.partial(join_kernel, heads),
+        kernel,
         in_specs=[pl.BlockSpec(memory_space=pltpu.SMEM), vmem, vmem]
-        + [anywhere] * (len(through) + len(after)),
-        out_specs=[anywhere] * len(through) + [vmem],
+        + [vmem] * len(through)
+        + [anywhere] * len(after),
+        out_specs=[vmem] * (len(through) + 1),
         out_shape=[message] * (len(through) + 1),
-        input_output_aliases={3 + i: i for i in range(len(through))},
-        compiler_params=pltpu.CompilerParams(vmem_limit_bytes=16 * MIB),
+        compiler_params=pltpu.CompilerParams(vmem_limit_bytes=8 * MIB),
         cost_estimate=pl.CostEstimate(
             flops=3 * rows * size, bytes_accessed=12 * rows * size, transcendentals=0
         ),
@@ -243,30 +232,44 @@
 def intra_kernel(
     first,
     heads,
-    mask_ref,
+    seg_ref,
     a_ref,
     gain_ref,
+    q_hbm,
+    k_hbm,
+    v_hbm,
+    g_hbm,
+    o_ref,
+    gate_ref,
     q_ref,
+    mask_ref,
     k_ref,
     v_ref,
-    g_hbm,
-    o_ref,
-    decay_ref,
-    gate_ref,
     g_ref,
     sems,
 ):
-    tokens = mask_ref.shape[0]
+    tokens = seg_ref.shape[1]
     size = q_ref.shape[1] // heads
-    block = min(tokens, 256)
+    block = min(tokens, 128)
+    copies = []
+    for p in range(0, heads, 2):
+        there, here = pl.ds((first + p) * size, 2 * size), pl.ds(p * size, 2 * size)
+        for i, (source, target) in enumerate(((q_hbm, q_ref), (k_hbm, k_ref), (v_hbm, v_ref))):
+            copies.append(
+                pltpu.make_async_copy(source.at[:, there], target.at[:, here], sems.at[i, p // 2])
+            )
     wide = pl.ds(first * size, heads * size)
-    copy = pltpu.make_async_copy(g_hbm.at[:, wide], g_ref, sems.at[0])
-    copy.start()
+    copies.append(pltpu.make_async_copy(g_hbm.at[:, wide], g_ref, sems.at[3, 0]))
+    for copy in copies:
+        copy.start()
+    make_mask(seg_ref, mask_ref)
     for j in range(heads):
+        if j % 2 == 0:
+            for copy in copies[3 * (j // 2) : 3 * (j // 2) + 3]:
+                copy.wait()
         columns = slice(j * size, (j + 1) * size)
         a_row = a_ref[first + j : first + j + 1, :] * 1.4426950408889634
         a_column = as_column(a_row, 128)
-        decay_ref[:, columns] = jnp.exp2(a_column)
         for start in range(0, tokens, block):
             here, upto = slice(start, start + block), slice(0, start + block)
             scores = lax.dot_general(
@@ -278,33 +281,36 @@
             o_ref[here, columns] = lax.dot_general(
                 probs, v_ref[upto, columns], NN, preferred_element_type=F32
             )
-    copy.wait()
+    copies[-1].wait()
     for j in range(heads):
         columns = slice(j * size, (j + 1) * size)
         half = 0.5 * gain_ref[:, (first + j) * size : (first + j + 1) * size]
-        gate_ref[:, columns] = half + half * jnp.tanh(0.5 * g_ref[:, columns].astype(F32))
-
-
-def intra(mask, a, gain, q, k, v, g, first, heads):
-    tokens, size = k.shape[0], k.shape[1] // heads
+        for start in range(0, tokens, block):
+            here = slice(start, start + block)
+            gate_ref[here, columns] = half + half * jnp.tanh(
+                0.5 * g_ref[here, columns].astype(F32)
+            )
+
+
+def intra(seg, a, gain, q, k, v, g, first, heads):
+    tokens, size = k.shape[0], k.shape[1] // a.shape[0]
     vmem = pl.BlockSpec(memory_space=pltpu.VMEM)
     return pl.pallas_call(
         functools.partial(intra_kernel, first, heads),
-        in_specs=[vmem] * 6 + [pl.BlockSpec(memory_space=pltpu.HBM)],
+        in_specs=[vmem] * 3 + [pl.BlockSpec(memory_space=pltpu.HBM)] * 4,
         out_specs=[vmem] * 3,
-        out_shape=[pltpu.VMEM((tokens, heads * size), F32)] * 3,
-        scratch_shapes=[
-            pltpu.VMEM((tokens, heads * size), BF16),
-            pltpu.SemaphoreType.DMA((1,)),
-        ],
-        compiler_params=pltpu.CompilerParams(vmem_limit_bytes=16 * MIB),
+        out_shape=[pltpu.VMEM((tokens, heads * size), dtype) for dtype in (F32, F32, BF16)],
+        scratch_shapes=[pltpu.VMEM((tokens, tokens), F32)]
+        + [pltpu.VMEM((tokens, heads * size), BF16)] * 3
+        + [pltpu.SemaphoreType.DMA((4, heads // 2))],
+        compiler_params=pltpu.CompilerParams(vmem_limit_bytes=8 * MIB),
         cost_estimate=pl.CostEstimate(
             flops=3 * tokens * tokens * heads * size,
             bytes_accessed=3 * MIB,
             transcendentals=tokens * tokens * heads,
         ),
         name="intra_span",
-    )(mask, a, gain, q, k, v, g)
+    )(seg, a, gain, q, k, v, g)
 
 
 def final_kernel(
@@ -316,16 +322,17 @@
     pair_ref,
     before_ref,
     o_ref,
-    decay_ref,
     gate_ref,
     q_ref,
+    a_ref,
     *rest,
 ):
     gated_hbm, snap_hbm, token_ref, gated_ref, snap_ref, sems = rest[-6:]
     token_ref[...] = jnp.zeros_like(token_ref)
     tokens, size = q_ref.shape[0], own_ref.shape[1]
+    block = min(tokens, 128)
     top = heads * size
-    second = order_ref[0] == 1
+    second = (order_ref[0] & 1) == 1
     ends = slice(top + heads, top + heads + 1)
     finals = slice(top, top + heads)
     own_end, pair_end, before_end = own_ref[ends, :], pair_ref[ends, :], before_ref[ends, :]
@@ -334,8 +341,9 @@
     bridged = jnp.where(pair_end == before_end, 1.0, 0.0)
     own_decay = jnp.exp(own_ref[finals, :]) * kept
     from_before = jnp.where(second, jnp.exp(pair_ref[finals, :]) * bridged, 1.0)
+    from_before = jnp.where(order_ref[0] >= 2, from_before, 0.0)
     from_pair = jnp.where(second, 1.0, 0.0)
-    valid = as_column(jnp.where(seg_ref[...].astype(F32) == previous[:, :1], 1.0, 0.0), size)
+    valid = seg_ref[...].astype(F32) == previous[:, :1]
     copies = []
     for j in range(heads):
         rows = columns = slice(j * size, (j + 1) * size)
@@ -344,16 +352,18 @@
         high = state.astype(BF16)
         low = (state - high.astype(F32)).astype(BF16)
         q = q_ref[:, columns]
-        inter = lax.dot_general(
-            jnp.concatenate([q, q], axis=1),
-            jnp.concatenate([high, low], axis=0),
-            NN,
-            preferred_element_type=F32,
-        )
-        mixed = o_ref[:, columns] + inter * (decay_ref[:, columns] * valid)
-        mean_square = jnp.mean(mixed * mixed, axis=1, keepdims=True)
-        gated = mixed * lax.rsqrt(mean_square + 1e-06) * gate_ref[:, columns]
-        gated_ref[:, columns] = gated.astype(BF16)
+        both = jnp.concatenate([high, low], axis=0)
+        decay = jnp.where(valid, jnp.exp(a_ref[first + j : first + j + 1, :]), 0.0)
+        decay = as_column(decay, size)
+        for start in range(0, tokens, block):
+            here = slice(start, start + block)
+            inter = lax.dot_general(
+                jnp.concatenate([q[here], q[here]], axis=1), both, NN, preferred_element_type=F32
+            )
+            mixed = o_ref[here, columns] + inter * decay[here]
+            mean_square = jnp.mean(mixed * mixed, axis=1, keepdims=True)
+            gated = mixed * lax.rsqrt(mean_square + 1e-06) * gate_ref[here, columns]
+            gated_ref[here, columns] = gated.astype(BF16)
         if j % 2 == 1 or j == heads - 1:
             begin = j - j % 2
             width = (j + 1 - begin) * size
@@ -369,8 +379,9 @@
         copy.wait()
 
 
-def finish(order, seg, own, pair, before, o, decay, gate, q, so_far, first, heads, total):
+def finish(order, seg, own, pair, before, o, gate, q, a, so_far, first, heads):
     tokens, size = q.shape[0], q.shape[1] // heads
+    total = a.shape[0]
     vmem, hbm = pl.BlockSpec(memory_space=pltpu.VMEM), pl.BlockSpec(memory_space=pltpu.HBM)
     return pl.pallas_call(
         functools.partial(final_kernel, first, heads),
@@ -387,14 +398,14 @@
             pltpu.SemaphoreType.DMA((2 * heads,)),
         ],
         input_output_aliases={9 + i: i for i in range(len(so_far))},
-        compiler_params=pltpu.CompilerParams(vmem_limit_bytes=16 * MIB),
+        compiler_params=pltpu.CompilerParams(vmem_limit_bytes=8 * MIB),
         cost_estimate=pl.CostEstimate(
             flops=4 * tokens * heads * size * size,
             bytes_accessed=4 * MIB,
             transcendentals=2 * tokens * heads * size,
         ),
         name="finish",
-    )(order, seg, own, pair, before, o, decay, gate, q, *so_far)
+    )(order, seg, own, pair, before, o, gate, q, a, *so_far)
 
 
 def shards(q, k, v, g, segment, decay_exponent, retention, norm_gain):
@@ -409,13 +420,14 @@
     far = lambda x: pltpu.with_memory_space_constraint(x, pltpu.HBM)
     q, k, v, g = far(q), far(k), far(v), far(g)
     gain = norm_gain.reshape(1, -1)
-    order = lax.rem(place, 2).astype(jnp.int32).reshape(1)
+    order = jnp.where(place >= 2, 2 + (place & 1), place & 1).astype(jnp.int32).reshape(1)
     swap = [(c, c ^ 1) for c in range(count)]
+    turn = [(c, (c + 2) % count) for c in range(count)]
 
     pair, before, inside, done = {}, {}, {}, {}
     result = ()
 
-    own0, a, w, seg, k0, v0 = first_message(
+    own0, a, w, seg = first_message(
         far(segment.reshape(1, tokens)),
         far(decay_exponent.reshape(1, heads)),
         far(retention),
@@ -426,13 +438,11 @@
     )
     own = [own0]
     pair[0] = lax.ppermute(own[0], "seq", swap)
-    mask, messages, k_near, v_near, q_near = prepare(seg, a, w, q, k, v, chunk)
-    k_near, v_near = [k0, *k_near], [v0, *v_near]
-    own += messages
+    own += rest_messages(seg, a, w, k, v, chunk)
     pair[1] = lax.ppermute(own[1], "seq", swap)
 
     def look_inside(i):
-        inside[i] = intra(mask, a, gain, q_near[i], k_near[i], v_near[i], g, firsts[i], chunk)
+        inside[i] = intra(seg, a, gain, q, k, v, g, firsts[i], chunk)
 
     look_inside(0)
     for i in range(last + 1):
@@ -444,16 +454,17 @@
         if through:
             own[i + 2] = through[0]
             pair[i + 2] = lax.ppermute(own[i + 2], "seq", swap)
-        before[i] = lax.ppermute(both, "seq", [(c, c + 2) for c in range(count - 2)])
+        before[i] = lax.ppermute(both, "seq", turn)
         window = 2
+        if window < reach:
+            before[i] = jnp.where(place >= 2, before[i], 0.0)
         while window < reach:
             past = lax.ppermute(before[i], "seq", [(c, c + window) for c in range(count - window)])
             (before[i],) = joined(jnp.ones((1,), jnp.int32), before[i], past, chunk)
             window *= 2
         for j in {last - 1: (0,), last: range(1, last + 1)}.get(i, ()):
             *result, done[j] = finish(
-                order, seg, own[j], pair[j], before[j], *inside[j], q_near[j], result, firsts[j],
-                chunk, heads,
+                order, seg, own[j], pair[j], before[j], *inside[j], a, result, firsts[j], chunk
             )
     return tuple(result)
 

time: 56.1 us -> 46 us (0.82)
  local copies, waits for them, and re-layouts: 9.28 us -> 0.01 us
  starting transfers between devices: 18 us -> 10.6 us
  waiting for transfers between devices: 0.02 us -> 6.49 us
  Pallas kernels: 27.3 us -> 27.9 us
    unnamed x38 -> x2, local copies, waits for them, and re-layouts: 9.28 us -> 0.01 us
    ppermute x4, starting transfers between devices: 12.9 us -> 5.46 us  [shards(): before[i] = lax.ppermute(both, 'seq', turn)]
    ppermute x4, waiting for transfers between devices: 0.01 us -> 6.48 us  [shards(): before[i] = lax.ppermute(both, 'seq', turn)]
    pallas_call x4, Pallas kernels: 10.2 us -> 15.2 us  [intra(): pl.pallas_call(functools.partial(intra_kernel, first, heads), in_specs=[v...]
    pallas_call x5, Pallas kernels: 5.69 us -> 2.61 us  [the longest x1 2.35 us: rest_messages(): pl.pallas_call(functools.partial(rest_kernel, chunk), in_specs=[pl.BlockS...]
    pallas_call x4, Pallas kernels: 9.82 us -> 8.4 us  [finish(): pl.pallas_call(functools.partial(final_kernel, first, heads), in_specs=[p...]
  transfers between devices with their start and end apart: 8 -> 8, of which waited for: 0 -> 2; matrix products, arithmetic and copies ran while one was open for 0% -> 0% of each run, Pallas kernels for 42% -> 52%
where the time goes in v3:
time: 46 us; the launch traced here: 45.8 us
  Pallas kernels  27.9 us (61%)
  starting transfers between devices  10.6 us (23%)
  waiting for transfers between devices  6.49 us (14%)
  between operations  0.76 us (2%)
    pallas_call x4, Pallas kernels, intra(): pl.pallas_call(functools.partial(intra_kernel, first, heads), in_specs=[v...  15.2 us
    pallas_call x4, Pallas kernels, finish(): pl.pallas_call(functools.partial(final_kernel, first, heads), in_specs=[p...  8.4 us
    ppermute x4, waiting for transfers between devices, shards(): before[i] = lax.ppermute(both, 'seq', turn)  6.48 us
    ppermute x4, starting transfers between devices, shards(): before[i] = lax.ppermute(both, 'seq', turn)  5.46 us
    ppermute x1, starting transfers between devices, shards(): pair[0] = lax.ppermute(own[0], 'seq', swap)  3 us
    pallas_call x1, Pallas kernels, rest_messages(): pl.pallas_call(functools.partial(rest_kernel, chunk), in_specs=[pl.BlockS...  2.35 us
    ppermute x2, starting transfers between devices, shards(): pair[i + 2] = lax.ppermute(own[i + 2], 'seq', swap)  2.09 us
    pallas_call x1, Pallas kernels, first_message(): pl.pallas_call(functools.partial(first_kernel, heads, chunk), in_specs=[p...  1.68 us
  transfers between devices with their start and end apart: 8, of which 2 were waited for; matrix products, arithmetic and copies ran while one was open for 0% of the time, Pallas kernels for 52%

profile of v3, /device:TPU:0, one launch (start us, length us, event | category | flops | bytes accessed | tf_op | source)
XLA Modules:
  0.0 45.8 jit_solution(1222856006822373729)
XLA Ops:
  0.6 1.7 %first_message.1 = (f32[520,128]{1,0:T(8,128)S(1)}, f32[16,512]{1,0:T(8,128)S(1)}, f32[16,512]{1,0:T(8,128)S(1)}, s32[1,512]{1,0:T(1,128)S(1)}) custom-call(s32[1,512]{1,0:T(1,128)} %bitcast.8, s32[1,16]{1,0:T(1,128)} %bitcast.9, f32[16,512]{1,0:T(8,128)} %keep_hbm.1, bf16[512,2048]{1,0:T(8,128)(2,1)} %k_hbm.11, bf16[512,2048]{1,0:T(8,128)(2,1)} %v_hbm.11), custom_call_target="tpu_custom_call" | custom-call | flops 67108864 | bytes 2097152 | tf_op jit(solution)/shard_map/first_message/pallas_call | solution.py:108
  2.3 3.0 %collective-permute-start.2 = (f32[520,128]{1,0:T(8,128)S(1)}, f32[520,128]{1,0:T(8,128)S(1)}, u32[]{:S(2)}, u32[]{:S(2)}) collective-permute-start(f32[520,128]{1,0:T(8,128)S(1)} %get-tuple-element.43.mine_ref.own_ref), channel_id=1, source_target_pairs={{0,2},{2,0},{4,6},{6,4},{8,10},{10,8},{12,14},{14,12},{1,3},{3,1},... | collective-permute-start | bytes 798728 | tf_op jit(solution)/shard_map/ppermute | solution.py:440
  5.3 2.3 %rest_messages.1 = (f32[520,128]{1,0:T(8,128)S(1)}, f32[520,128]{1,0:T(8,128)S(1)}, f32[520,128]{1,0:T(8,128)S(1)}) custom-call(s32[1,512]{1,0:T(1,128)S(1)} %get-tuple-element.34.seg_ref, f32[16,512]{1,0:T(8,128)S(1)} %get-tuple-element.35.a_ref, f32[16,512]{1,0:T(8,128)S(1)} %get-tuple-element.36.w_ref, bf16[512,2048]{1,0:T(8,128)(2,1)} %k_hbm.11, ...), custom_call_target="tpu_custom_call" | custom-call | flops 268435456 | bytes 4194304 | tf_op jit(solution)/shard_map/rest_messages/pallas_call | solution.py:159
  7.7 0.1 collective-permute-start
  7.8 3.8 %intra_span.4 = (f32[512,512]{1,0:T(8,128)S(1)}, f32[512,512]{1,0:T(8,128)S(1)}, bf16[512,512]{1,0:T(8,128)(2,1)S(1)}) custom-call(s32[1,512]{1,0:T(1,128)S(1)} %get-tuple-element.34.seg_ref, f32[16,512]{1,0:T(8,128)S(1)} %get-tuple-element.35.a_ref, f32[1,2048]{1,0:T(1,128)S(1)} %bitcast.4, bf16[512,2048]{1,0:T(8,128)(2,1)} %q_hbm.7, ...), custom_call_target="tpu_custom_call" | custom-call | flops 402653184 | bytes 3145728 | tf_op jit(solution)/shard_map/intra_span/pallas_call | solution.py:298
  11.6 3.8 %intra_span.7 = (f32[512,512]{1,0:T(8,128)S(1)}, f32[512,512]{1,0:T(8,128)S(1)}, bf16[512,512]{1,0:T(8,128)(2,1)S(1)}) custom-call(s32[1,512]{1,0:T(1,128)S(1)} %get-tuple-element.34.seg_ref, f32[16,512]{1,0:T(8,128)S(1)} %get-tuple-element.35.a_ref, f32[1,2048]{1,0:T(1,128)S(1)} %bitcast.5, bf16[512,2048]{1,0:T(8,128)(2,1)} %q_hbm.7, ...), custom_call_target="tpu_custom_call" | custom-call | flops 402653184 | bytes 3145728 | tf_op jit(solution)/shard_map/intra_span/pallas_call | solution.py:298
  15.4 0.1 join_windows.5
  15.5 2.1 %collective-permute-start.3 = (f32[520,128]{1,0:T(8,128)S(1)}, f32[520,128]{1,0:T(8,128)S(1)}, u32[]{:S(2)}, u32[]{:S(2)}) collective-permute-start(f32[520,128]{1,0:T(8,128)S(1)} %get-tuple-element.46), channel_id=1, source_target_pairs={{0,4},{2,6},{4,8},{6,10},{8,12},{10,14},{12,0},{14,2},{1,5},{3,7},... | collective-permute-start | bytes 798728 | tf_op jit(solution)/shard_map/ppermute | solution.py:457
  17.6 1.5 %collective-permute-start.5 = (f32[520,128]{1,0:T(8,128)S(1)}, f32[520,128]{1,0:T(8,128)S(1)}, u32[]{:S(2)}, u32[]{:S(2)}) collective-permute-start(f32[520,128]{1,0:T(8,128)S(1)} %get-tuple-element.52.mine_ref.own_ref), channel_id=1, source_target_pairs={{0,2},{2,0},{4,6},{6,4},{8,10},{10,8},{12,14},{14,12},{1,3},{3,1},... | collective-permute-start | bytes 798728 | tf_op jit(solution)/shard_map/ppermute | solution.py:456
  19.1 3.8 %intra_span.5 = (f32[512,512]{1,0:T(8,128)S(1)}, f32[512,512]{1,0:T(8,128)S(1)}, bf16[512,512]{1,0:T(8,128)(2,1)S(1)}) custom-call(s32[1,512]{1,0:T(1,128)S(1)} %get-tuple-element.34.seg_ref, f32[16,512]{1,0:T(8,128)S(1)} %get-tuple-element.35.a_ref, f32[1,2048]{1,0:T(1,128)S(1)} %bitcast.6, bf16[512,2048]{1,0:T(8,128)(2,1)} %q_hbm.7, ...), custom_call_target="tpu_custom_call" | custom-call | flops 402653184 | bytes 3145728 | tf_op jit(solution)/shard_map/intra_span/pallas_call | solution.py:298
  22.9 0.1 join_windows.4
  23.0 0.6 %collective-permute-start.1 = (f32[520,128]{1,0:T(8,128)S(1)}, f32[520,128]{1,0:T(8,128)S(1)}, u32[]{:S(2)}, u32[]{:S(2)}) collective-permute-start(f32[520,128]{1,0:T(8,128)S(1)} %get-tuple-element.41.mine_ref.own_ref), channel_id=1, source_target_pairs={{0,2},{2,0},{4,6},{6,4},{8,10},{10,8},{12,14},{14,12},{1,3},{3,1},... | collective-permute-start | bytes 798728 | tf_op jit(solution)/shard_map/ppermute | solution.py:456
  23.6 1.6 %collective-permute-start.7 = (f32[520,128]{1,0:T(8,128)S(1)}, f32[520,128]{1,0:T(8,128)S(1)}, u32[]{:S(2)}, u32[]{:S(2)}) collective-permute-start(f32[520,128]{1,0:T(8,128)S(1)} %get-tuple-element.55), channel_id=1, source_target_pairs={{0,4},{2,6},{4,8},{6,10},{8,12},{10,14},{12,0},{14,2},{1,5},{3,7},... | collective-permute-start | bytes 798728 | tf_op jit(solution)/shard_map/ppermute | solution.py:457
  25.2 3.8 %intra_span.6 = (f32[512,512]{1,0:T(8,128)S(1)}, f32[512,512]{1,0:T(8,128)S(1)}, bf16[512,512]{1,0:T(8,128)(2,1)S(1)}) custom-call(s32[1,512]{1,0:T(1,128)S(1)} %get-tuple-element.34.seg_ref, f32[16,512]{1,0:T(8,128)S(1)} %get-tuple-element.35.a_ref, f32[1,2048]{1,0:T(1,128)S(1)} %bitcast.7, bf16[512,2048]{1,0:T(8,128)(2,1)} %q_hbm.7, ...), custom_call_target="tpu_custom_call" | custom-call | flops 402653184 | bytes 3145728 | tf_op jit(solution)/shard_map/intra_span/pallas_call | solution.py:298
  29.0 0.1 join_windows.7
  29.1 1.6 %collective-permute-start.6 = (f32[520,128]{1,0:T(8,128)S(1)}, f32[520,128]{1,0:T(8,128)S(1)}, u32[]{:S(2)}, u32[]{:S(2)}) collective-permute-start(f32[520,128]{1,0:T(8,128)S(1)} %join_windows.7), channel_id=1, source_target_pairs={{0,4},{2,6},{4,8},{6,10},{8,12},{10,14},{12,0},{14,2},{1,5},{3,7},... | collective-permute-start | bytes 798728 | tf_op jit(solution)/shard_map/ppermute | solution.py:457
  30.7 1.7 %finish.4 = (bf16[512,2048]{1,0:T(8,128)(2,1)}, f32[1,16,128,128]{3,2,1,0:T(8,128)}, f32[8,128]{1,0:T(8,128)S(1)}) custom-call(s32[1]{0:T(128)} %bitcast.order_ref, s32[1,512]{1,0:T(1,128)S(1)} %get-tuple-element.34.seg_ref, f32[520,128]{1,0:T(8,128)S(1)} %get-tuple-element.43.mine_ref.own_ref, f32[520,128]{1,0:T(8,128)S(1)} %collective-permute-done.2.other_ref.pair_ref, ...), custom_call_target="tpu_custom_call" | custom-call | flops 134217728 | bytes 4194304 | tf_op jit(solution)/shard_map/finish/pallas_call | solution.py:386
  32.4 0.1 join_windows.6
  32.4 0.1 collective-permute-start.4
  32.5 2.2 %finish.5 = (bf16[512,2048]{1,0:T(8,128)(2,1)}, f32[1,16,128,128]{3,2,1,0:T(8,128)}, f32[8,128]{1,0:T(8,128)}) custom-call(s32[1]{0:T(128)} %bitcast.order_ref, s32[1,512]{1,0:T(1,128)S(1)} %get-tuple-element.34.seg_ref, f32[520,128]{1,0:T(8,128)S(1)} %get-tuple-element.37.mine_ref.own_ref, ...), custom_call_target="tpu_custom_call", output_to_operand_aliasing={{0}: (9, {}), {1}: (10, {})} | custom-call | flops 134217728 | bytes 4194304 | tf_op jit(solution)/shard_map/finish/pallas_call | solution.py:386
  34.8 5.4 %collective-permute-done.6.before_ref = f32[520,128]{1,0:T(8,128)S(1)} collective-permute-done((f32[520,128]{1,0:T(8,128)S(1)}, f32[520,128]{1,0:T(8,128)S(1)}, u32[]{:S(2)}, u32[]{:S(2)}) %collective-permute-start.6) | collective-permute-done | bytes 266272 | tf_op jit(solution)/shard_map/ppermute | solution.py:457
  40.2 2.3 %finish.6 = (bf16[512,2048]{1,0:T(8,128)(2,1)}, f32[1,16,128,128]{3,2,1,0:T(8,128)}, f32[8,128]{1,0:T(8,128)}) custom-call(s32[1]{0:T(128)} %bitcast.order_ref, s32[1,512]{1,0:T(1,128)S(1)} %get-tuple-element.34.seg_ref, f32[520,128]{1,0:T(8,128)S(1)} %get-tuple-element.52.mine_ref.own_ref, ...), custom_call_target="tpu_custom_call", output_to_operand_aliasing={{0}: (9, {}), {1}: (10, {})} | custom-call | flops 134217728 | bytes 4194304 | tf_op jit(solution)/shard_map/finish/pallas_call | solution.py:386
  42.5 1.0 %collective-permute-done.4.before_ref = f32[520,128]{1,0:T(8,128)S(1)} collective-permute-done((f32[520,128]{1,0:T(8,128)S(1)}, f32[520,128]{1,0:T(8,128)S(1)}, u32[]{:S(2)}, u32[]{:S(2)}) %collective-permute-start.4) | collective-permute-done | bytes 266272 | tf_op jit(solution)/shard_map/ppermute | solution.py:457
  43.5 2.2 %finish.7 = (bf16[512,2048]{1,0:T(8,128)(2,1)}, f32[1,16,128,128]{3,2,1,0:T(8,128)}, f32[8,128]{1,0:T(8,128)}) custom-call(s32[1]{0:T(128)} %bitcast.order_ref, s32[1,512]{1,0:T(1,128)S(1)} %get-tuple-element.34.seg_ref, f32[520,128]{1,0:T(8,128)S(1)} %get-tuple-element.41.mine_ref.own_ref, ...), custom_call_target="tpu_custom_call", output_to_operand_aliasing={{0}: (9, {}), {1}: (10, {})} | custom-call | flops 134217728 | bytes 4194304 | tf_op jit(solution)/shard_map/finish/pallas_call | solution.py:386
  (8 shorter events, 0.0 us)
Async XLA Ops:
  2.3 13.1 %collective-permute-start.2 = (f32[520,128]{1,0:T(8,128)S(1)}, f32[520,128]{1,0:T(8,128)S(1)}, u32[]{:S(2)}, u32[]{:S(2)}) collective-permute-start(f32[520,128]{1,0:T(8,128)S(1)} %get-tuple-element.43.mine_ref.own_ref), channel_id=1, source_target_pairs={{0,2},{2,0},{4,6},{6,4},{8,10},{10,8},{12,14},{14,12},{1,3},{3,1},... | collective-permute-start | bytes 798728 | tf_op jit(solution)/shard_map/ppermute | solution.py:440
  5.3 2.4 %copy-start = (f32[2048]{0:T(1024)S(1)}, f32[2048]{0:T(1024)}, u32[]{:S(2)}) copy-start(f32[2048]{0:T(1024)} %param.15) | copy-start | bytes 24580
  7.7 15.2 %collective-permute-start = (f32[520,128]{1,0:T(8,128)S(1)}, f32[520,128]{1,0:T(8,128)S(1)}, u32[]{:S(2)}, u32[]{:S(2)}) collective-permute-start(f32[520,128]{1,0:T(8,128)S(1)} %get-tuple-element.37.mine_ref.own_ref), channel_id=1, source_target_pairs={{0,2},{2,0},{4,6},{6,4},{8,10},{10,8},{12,14},{14,12},{1,3},{3,1},... | collective-permute-start | bytes 798728 | tf_op jit(solution)/shard_map/ppermute | solution.py:442
  15.5 15.2 %collective-permute-start.3 = (f32[520,128]{1,0:T(8,128)S(1)}, f32[520,128]{1,0:T(8,128)S(1)}, u32[]{:S(2)}, u32[]{:S(2)}) collective-permute-start(f32[520,128]{1,0:T(8,128)S(1)} %get-tuple-element.46), channel_id=1, source_target_pairs={{0,4},{2,6},{4,8},{6,10},{8,12},{10,14},{12,0},{14,2},{1,5},{3,7},... | collective-permute-start | bytes 798728 | tf_op jit(solution)/shard_map/ppermute | solution.py:457
  17.6 11.4 %collective-permute-start.5 = (f32[520,128]{1,0:T(8,128)S(1)}, f32[520,128]{1,0:T(8,128)S(1)}, u32[]{:S(2)}, u32[]{:S(2)}) collective-permute-start(f32[520,128]{1,0:T(8,128)S(1)} %get-tuple-element.52.mine_ref.own_ref), channel_id=1, source_target_pairs={{0,2},{2,0},{4,6},{6,4},{8,10},{10,8},{12,14},{14,12},{1,3},{3,1},... | collective-permute-start | bytes 798728 | tf_op jit(solution)/shard_map/ppermute | solution.py:456
  23.0 9.3 %collective-permute-start.1 = (f32[520,128]{1,0:T(8,128)S(1)}, f32[520,128]{1,0:T(8,128)S(1)}, u32[]{:S(2)}, u32[]{:S(2)}) collective-permute-start(f32[520,128]{1,0:T(8,128)S(1)} %get-tuple-element.41.mine_ref.own_ref), channel_id=1, source_target_pairs={{0,2},{2,0},{4,6},{6,4},{8,10},{10,8},{12,14},{14,12},{1,3},{3,1},... | collective-permute-start | bytes 798728 | tf_op jit(solution)/shard_map/ppermute | solution.py:456
  23.6 8.9 %collective-permute-start.7 = (f32[520,128]{1,0:T(8,128)S(1)}, f32[520,128]{1,0:T(8,128)S(1)}, u32[]{:S(2)}, u32[]{:S(2)}) collective-permute-start(f32[520,128]{1,0:T(8,128)S(1)} %get-tuple-element.55), channel_id=1, source_target_pairs={{0,4},{2,6},{4,8},{6,10},{8,12},{10,14},{12,0},{14,2},{1,5},{3,7},... | collective-permute-start | bytes 798728 | tf_op jit(solution)/shard_map/ppermute | solution.py:457
  29.1 11.2 %collective-permute-start.6 = (f32[520,128]{1,0:T(8,128)S(1)}, f32[520,128]{1,0:T(8,128)S(1)}, u32[]{:S(2)}, u32[]{:S(2)}) collective-permute-start(f32[520,128]{1,0:T(8,128)S(1)} %join_windows.7), channel_id=1, source_target_pairs={{0,4},{2,6},{4,8},{6,10},{8,12},{10,14},{12,0},{14,2},{1,5},{3,7},... | collective-permute-start | bytes 798728 | tf_op jit(solution)/shard_map/ppermute | solution.py:457
  32.4 11.1 %collective-permute-start.4 = (f32[520,128]{1,0:T(8,128)S(1)}, f32[520,128]{1,0:T(8,128)S(1)}, u32[]{:S(2)}, u32[]{:S(2)}) collective-permute-start(f32[520,128]{1,0:T(8,128)S(1)} %join_windows.6), channel_id=1, source_target_pairs={{0,4},{2,6},{4,8},{6,10},{8,12},{10,14},{12,0},{14,2},{1,5},{3,7},... | collective-permute-start | bytes 798728 | tf_op jit(solution)/shard_map/ppermute | solution.py:457
